TPU v7x, 128 devices: a whole 4x4x4 slice. The times are simulated.
128 devices in a mesh: ta: 16 (over y, x_hi, core), gz: 8 (over z, x_lo).
Axes of the slice: x: 4 (x_hi: 2, x_lo: 2; x = x_hi * 2 + x_lo), y: 4, z: 4, core: 2. Of those that a mesh axis runs over, the one named last changes fastest.
Arguments:
- restricted: float32 [16, 96, 16384], P('gz', None, 'ta'), may hold values from -6 to 6
- mass_terms: float32 [96, 16384], P(None, ('ta', 'gz')), may hold values from 2 to 4
- clover_blocks: bfloat16 [96, 96, 16384], P(None, None, ('ta', 'gz')), may hold values from -0.4375 to 0.4375
- hop_links: bfloat16 [8, 96, 96, 16384], P(None, None, None, ('ta', 'gz')), may hold values from -0.21875 to 0.21875
Outputs:
- solution: float32 [16, 96, 16384], P('gz', None, 'ta')
- residual: float32 [16, 96, 16384], P(None, None, ('ta', 'gz'))
All inputs are finite; a program needn't handle non-finite values.
Results may differ from a plain program's by a relative error of at most 0.013.
Values may be sent and summed in bfloat16 or wider, within the bound.
A program may use at most 128 MiB of HBM per device.

v0:
```python
import jax
import jax.numpy as jnp
from jax import lax
from jax.sharding import PartitionSpec as P

NC = 96
LX = 4
LY = 4
CT = 2
CZ = 4
ITERS = 4


def padded_2(block, sides, width):
    for axis, dim in sides:
        count = lax.axis_size(axis)
        forward = [(i, i + 1) for i in range(count - 1)]
        forward.append((count - 1, 0))
        backward = [(target, source) for source, target in forward]
        low = lax.ppermute(
            lax.slice_in_dim(block, block.shape[dim] - width, None, axis=dim), axis, forward
        )
        high = lax.ppermute(lax.slice_in_dim(block, 0, width, axis=dim), axis, backward)
        block = jnp.concatenate([low, block, high], axis=dim)
    return block


def inner(left, right):
    return jnp.sum(left * right, axis=(1, 2))


def coarse_apply(vectors, mass_terms, clover_blocks, hop_links):
    count = vectors.shape[0]
    halved = vectors.astype(jnp.bfloat16)
    lattice = halved.reshape(count, NC, CT, CZ, LX, LY)

    def hop_term(number, shifted):
        return jnp.einsum(
            "ijs,rjs->ris",
            hop_links[number],
            shifted.reshape(count, NC, -1),
            preferred_element_type=jnp.float32,
        )

    result = mass_terms[None] * vectors + jnp.einsum(
        "ijs,rjs->ris", clover_blocks, halved, preferred_element_type=jnp.float32
    )
    result = result + hop_term(0, jnp.roll(lattice, -1, 4)) + hop_term(1, jnp.roll(lattice, 1, 4))
    result = result + hop_term(2, jnp.roll(lattice, -1, 5)) + hop_term(3, jnp.roll(lattice, 1, 5))
    padded = padded_2(lattice, (("ta", 2), ("gz", 3)), 1)
    result = result + hop_term(4, padded[:, :, 1:-1, 2:]) + hop_term(5, padded[:, :, 1:-1, :-2])
    result = result + hop_term(6, padded[:, :, 2:, 1:-1]) + hop_term(7, padded[:, :, :-2, 1:-1])
    return result


def shards(restricted, mass_terms, clover_blocks, hop_links):
    residual = lax.all_to_all(
        restricted.astype(jnp.bfloat16), "gz", split_axis=2, concat_axis=0, tiled=True
    ).astype(restricted.dtype)
    solution = jnp.zeros_like(residual)
    images = []
    searches = []
    for number in range(ITERS):
        image = coarse_apply(residual, mass_terms, clover_blocks, hop_links)
        image_out = image
        search = residual
        if number > 0:
            weights = lax.psum(
                jnp.stack([inner(earlier, image) for earlier in images]), ("ta", "gz")
            )
            for earlier in range(number):
                weight = weights[earlier][:, None, None]
                image_out = image_out - weight * images[earlier]
                search = search - weight * searches[earlier]
        squared = lax.psum(inner(image_out, image_out), ("ta", "gz"))
        length = jnp.sqrt(squared + 1e-06)[:, None, None]
        image_out = image_out / length
        search = search / length
        alpha = lax.psum(inner(image_out, residual), ("ta", "gz"))[:, None, None]
        solution = solution + alpha * search
        residual = residual - alpha * image_out
        images.append(image_out)
        searches.append(search)
    solution_out = lax.all_to_all(
        solution.astype(jnp.bfloat16), "gz", split_axis=0, concat_axis=2, tiled=True
    ).astype(solution.dtype)
    return (solution_out, residual)


def solution(mesh):
    return jax.shard_map(
        shards,
        mesh=mesh,
        in_specs=(
            P("gz", None, "ta"),
            P(None, ("ta", "gz")),
            P(None, None, ("ta", "gz")),
            P(None, None, None, ("ta", "gz")),
        ),
        out_specs=(P("gz", None, "ta"), P(None, None, ("ta", "gz"))),
        check_vma=False,
    )
```

profile of v0, /device:TPU:1, one launch (start us, length us, event | category | flops | bytes accessed | tf_op | source)
XLA Modules:
  0.0 956.6 jit_solution(10320681381625894540)
XLA Ops:
  2.9 6.8 all-to-all-start
  9.7 13.1 %fusion.265 = (bf16[1,96,96,128]{3,2,1,0:T(8,128)(2,1)S(1)}, bf16[1,96,96,128]{3,2,1,0:T(8,128)(2,1)}, bf16[1,96,96,128]{3,2,1,0:T(8,128)(2,1)}, bf16[1,96,96,12...) fusion(bf16[8,96,96,128]{3,2,1,0:T(8,128)(2,1)} %param.7), kind=kLoop, calls=%fused_computation.241 | loop fusion | bytes 37748736 | tf_op jit(solution)/shard_map/slice | solution.py:40
  22.8 4.8 copy.59
  27.6 4.8 copy.60
  32.4 4.8 copy.61
  37.2 4.8 copy.43
  42.1 4.8 copy.58
  46.9 4.8 copy.63
  51.7 4.8 copy.64
  56.5 4.9 copy.65
  61.3 3.2 copy.62
  65.4 3.4 collective-permute-start
  76.9 3.9 collective-permute-start.2
  84.2 7.2 collective-permute-done.3
  99.3 66.4 %psum.77 = f32[16]{0:T(128)S(1)} all-reduce(f32[16]{0:T(128)S(1)} %get-tuple-element.102), channel_id=1, replica_groups=mesh['ta'=16,'gz'=8] {'ta','gz'}, use_global_device_ids=true, to_apply=%region_1.2 | all-reduce | flops 16 | bytes 128 | tf_op jit(solution)/shard_map/psum | solution.py:75
  166.1 63.0 %psum.78 = f32[16]{0:T(128)S(1)} all-reduce(f32[16]{0:T(128)S(1)} %fusion.260), channel_id=1, replica_groups=mesh['ta'=16,'gz'=8] {'ta','gz'}, use_global_device_ids=true, to_apply=%region_3.4 | all-reduce | flops 16 | bytes 128 | tf_op jit(solution)/shard_map/psum | solution.py:79
  238.3 2.0 collective-permute-start.4
  243.6 5.4 collective-permute-done.5
  252.7 3.0 collective-permute-done.6
  255.7 4.9 collective-permute-done.7
  268.6 66.6 %psum.79 = f32[16]{0:T(128)S(1)} all-reduce(f32[16]{0:T(128)S(1)} %get-tuple-element.104), channel_id=1, replica_groups=mesh['ta'=16,'gz'=8] {'ta','gz'}, use_global_device_ids=true, to_apply=%region_5.6 | all-reduce | flops 16 | bytes 128 | tf_op jit(solution)/shard_map/psum | solution.py:68
  335.6 62.6 %psum.80 = f32[16]{0:T(128)S(1)} all-reduce(f32[16]{0:T(128)S(1)} %multiply_reduce_fusion.10), channel_id=1, replica_groups=mesh['ta'=16,'gz'=8] {'ta','gz'}, use_global_device_ids=true, to_apply=%region_7.8 | all-reduce | flops 16 | bytes 128 | tf_op jit(solution)/shard_map/psum | solution.py:75
  400.0 64.1 %psum.81 = f32[16]{0:T(128)S(1)} all-reduce(f32[16]{0:T(128)S(1)} %get-tuple-element.21), channel_id=1, replica_groups=mesh['ta'=16,'gz'=8] {'ta','gz'}, use_global_device_ids=true, to_apply=%region_9.10 | all-reduce | flops 16 | bytes 128 | tf_op jit(solution)/shard_map/psum | solution.py:79
  464.8 1.9 copy-done.34
  472.2 2.1 collective-permute-start.8
  477.6 4.4 collective-permute-done.9
  485.5 2.0 collective-permute-done.10
  487.5 9.3 collective-permute-done.11
  502.8 2.9 multiply_reduce_fusion.8
  505.7 63.7 %psum.82 = f32[2,16]{1,0:T(2,128)S(1)} all-reduce(f32[2,16]{1,0:T(2,128)S(1)} %pad_maximum_fusion.61), channel_id=1, replica_groups=mesh['ta'=16,'gz'=8] {'ta','gz'}, use_global_device_ids=true, to_apply=%region_12.13 | all-reduce | flops 32 | bytes 256 | tf_op jit(solution)/shard_map/psum | solution.py:68
  569.4 2.6 multiply_reduce_fusion.6
  572.0 62.6 %psum.83 = f32[16]{0:T(128)S(1)} all-reduce(f32[16]{0:T(128)S(1)} %get-tuple-element.17), channel_id=1, replica_groups=mesh['ta'=16,'gz'=8] {'ta','gz'}, use_global_device_ids=true, to_apply=%region_14.15 | all-reduce | flops 16 | bytes 128 | tf_op jit(solution)/shard_map/psum | solution.py:75
  634.7 1.9 multiply_reduce_fusion.5
  636.6 64.3 %psum.84 = f32[16]{0:T(128)S(1)} all-reduce(f32[16]{0:T(128)S(1)} %multiply_reduce_fusion.5), channel_id=1, replica_groups=mesh['ta'=16,'gz'=8] {'ta','gz'}, use_global_device_ids=true, to_apply=%region_16.17 | all-reduce | flops 16 | bytes 128 | tf_op jit(solution)/shard_map/psum | solution.py:79
  703.1 1.8 copy-done.35
  710.5 2.1 collective-permute-start.12
  715.9 4.3 collective-permute-done.13
  723.6 2.0 collective-permute-done.14
  725.6 9.5 collective-permute-done.15
  741.3 2.9 multiply_reduce_fusion.4
  744.2 63.7 %psum.85 = f32[3,16]{1,0:T(4,128)S(1)} all-reduce(f32[3,16]{1,0:T(4,128)S(1)} %pad_maximum_fusion.60), channel_id=1, replica_groups=mesh['ta'=16,'gz'=8] {'ta','gz'}, use_global_device_ids=true, to_apply=%region_20.21 | all-reduce | flops 48 | bytes 384 | tf_op jit(solution)/shard_map/psum | solution.py:68
  807.9 3.1 multiply_reduce_fusion.1
  811.0 62.6 %psum.86 = f32[16]{0:T(128)S(1)} all-reduce(f32[16]{0:T(128)S(1)} %get-tuple-element.13), channel_id=1, replica_groups=mesh['ta'=16,'gz'=8] {'ta','gz'}, use_global_device_ids=true, to_apply=%region_22.23 | all-reduce | flops 16 | bytes 128 | tf_op jit(solution)/shard_map/psum | solution.py:75
  873.6 1.9 multiply_reduce_fusion
  875.5 64.1 %psum.87 = f32[16]{0:T(128)S(1)} all-reduce(f32[16]{0:T(128)S(1)} %multiply_reduce_fusion), channel_id=1, replica_groups=mesh['ta'=16,'gz'=8] {'ta','gz'}, use_global_device_ids=true, to_apply=%region_24.25 | all-reduce | flops 16 | bytes 128 | tf_op jit(solution)/shard_map/psum | solution.py:79
  939.6 3.0 multiply_subtract_fusion
  943.8 3.5 all-to-all-start.1
  948.6 6.5 all-to-all-done.1
  (195 shorter events, 91.7 us)
Async XLA Ops:
  2.9 61.7 %all-to-all-start = ((bf16[2,96,1024]{1,0,2:T(2,128)(2,1)}), bf16[2,96,1024]{1,0,2:T(2,128)(2,1)S(1)}, u32[]{:S(2)}, u32[]{:S(2)}) async-start(bf16[2,96,1024]{1,0,2:T(2,128)(2,1)} %copy.41), calls=%async_computation | async-start | bytes 1048576 | tf_op jit(solution)/shard_map/all_to_all | solution.py:57
  37.2 4.8 copy-start.40
  65.1 3.8 copy-start.24
  65.4 10.9 %collective-permute-start = (bf16[16,96,1,4,4,4]{1,0,5,4,3,2:T(8,128)(2,1)S(1)}, bf16[16,96,1,4,4,4]{1,0,5,4,3,2:T(8,128)(2,1)S(1)}, u32[]{:S(2)}, u32[]{:S(2)}) collective-permute-start(bf16[16,96,1,4,4,4]{1,0,5,4,3,2:T(8,128)(2,1)S(1)} %get-tuple-element.96), channel_id=1, source_target_pairs={{0,8},{8,16},{16,24},{24,32},{32,40},{40,48},{48,56},{56,64},{64,7... | collective-permute-start | bytes 589832 | tf_op jit(solution)/shard_map/ppermute | solution.py:20
  68.7 8.1 collective-permute-start.1
  68.9 2.0 copy-start.20
  70.7 2.0 copy-start.32
  74.5 6.5 copy-start.12
  76.9 7.2 collective-permute-start.2
  80.9 10.6 %collective-permute-start.3 = (bf16[16,96,4,1,4,4]{1,0,5,4,3,2:T(8,128)(2,1)S(1)}, bf16[16,96,4,1,4,4]{1,0,5,4,3,2:T(8,128)(2,1)S(1)}, u32[]{:S(2)}, u32[]{:S(2)}) collective-permute-start(bf16[16,96,4,1,4,4]{1,0,5,4,3,2:T(8,128)(2,1)S(1)} %get-tuple-element.48), channel_id=1, source_target_pairs={{0,1},{1,2},{2,3},{3,4},{4,5},{5,6},{6,7},{7,0},{8,9},{9,10},{10,1... | collective-permute-start | bytes 589832 | tf_op jit(solution)/shard_map/ppermute | solution.py:20
  82.8 9.1 copy-start.8
  93.6 1.9 copy-start
  95.5 1.9 copy-start.28
  233.1 3.4 copy-start.21
  236.6 3.8 copy-start.17
  238.3 5.3 collective-permute-start.4
  240.3 8.7 collective-permute-start.5
  240.4 10.6 %copy-start.13 = (bf16[1,96,96,128]{2,1,3,0:T(8,128)(2,1)S(1)}, bf16[1,96,96,128]{2,1,3,0:T(8,128)(2,1)}, u32[]{:S(2)}) copy-start(bf16[1,96,96,128]{2,1,3,0:T(8,128)(2,1)} %copy.58) | copy-start | bytes 7077892
  249.1 6.7 collective-permute-start.6
  250.3 10.4 %collective-permute-start.7 = (bf16[16,96,4,1,4,4]{1,0,5,4,3,2:T(8,128)(2,1)S(1)}, bf16[16,96,4,1,4,4]{1,0,5,4,3,2:T(8,128)(2,1)S(1)}, u32[]{:S(2)}, u32[]{:S(2)}) collective-permute-start(bf16[16,96,4,1,4,4]{1,0,5,4,3,2:T(8,128)(2,1)S(1)} %get-tuple-element.44), channel_id=1, source_target_pairs={{0,1},{1,2},{2,3},{3,4},{4,5},{5,6},{6,7},{7,0},{8,9},{9,10},{10,1... | collective-permute-start | bytes 589832 | tf_op jit(solution)/shard_map/ppermute | solution.py:20
  252.7 8.4 copy-start.9
  262.9 1.9 copy-start.1
  264.8 1.9 copy-start.29
  268.5 129.7 %copy-start.39 = (f32[16,96,128]{1,0,2:T(8,128)}, f32[16,96,128]{1,0,2:T(8,128)S(1)}, u32[]{:S(2)}) copy-start(f32[16,96,128]{1,0,2:T(8,128)S(1)} %get-tuple-element.105) | copy-start | bytes 2359300
  464.4 4.0 copy-start.36
  464.4 2.3 copy-start.34
  470.5 4.1 copy-start.18
  472.2 5.4 collective-permute-start.8
  474.3 7.7 collective-permute-start.9
  474.6 9.1 copy-start.14
  482.2 5.3 collective-permute-start.10
  483.6 13.1 %collective-permute-start.11 = (bf16[16,96,4,1,4,4]{1,0,5,4,3,2:T(8,128)(2,1)S(1)}, bf16[16,96,4,1,4,4]{1,0,5,4,3,2:T(8,128)(2,1)S(1)}, u32[]{:S(2)}, u32[]{:S(2)}) collective-permute-start(bf16[16,96,4,1,4,4]{1,0,5,4,3,2:T(8,128)(2,1)S(1)} %get-tuple-element.40), channel_id=1, source_target_pairs={{0,1},{1,2},{2,3},{3,4},{4,5},{5,6},{6,7},{7,0},{8,9},{9,10},{10,1... | collective-permute-start | bytes 589832 | tf_op jit(solution)/shard_map/ppermute | solution.py:20
  485.5 11.8 %copy-start.10 = (bf16[1,96,96,128]{2,1,3,0:T(8,128)(2,1)S(1)}, bf16[1,96,96,128]{2,1,3,0:T(8,128)(2,1)}, u32[]{:S(2)}) copy-start(bf16[1,96,96,128]{2,1,3,0:T(8,128)(2,1)} %copy.63) | copy-start | bytes 7077892
  499.0 1.9 copy-start.2
  500.9 1.9 copy-start.30
  702.7 4.0 copy-start.38
  702.7 2.3 copy-start.35
  708.7 4.0 copy-start.19
  710.5 5.4 collective-permute-start.12
  712.6 7.6 collective-permute-start.13
  712.7 9.1 copy-start.15
  720.3 5.3 collective-permute-start.14
  721.8 13.3 %collective-permute-start.15 = (bf16[16,96,4,1,4,4]{1,0,5,4,3,2:T(8,128)(2,1)S(1)}, bf16[16,96,4,1,4,4]{1,0,5,4,3,2:T(8,128)(2,1)S(1)}, u32[]{:S(2)}, u32[]{:S(2)}) collective-permute-start(bf16[16,96,4,1,4,4]{1,0,5,4,3,2:T(8,128)(2,1)S(1)} %get-tuple-element.36), channel_id=1, source_target_pairs={{0,1},{1,2},{2,3},{3,4},{4,5},{5,6},{6,7},{7,0},{8,9},{9,10},{10,1... | collective-permute-start | bytes 589832 | tf_op jit(solution)/shard_map/ppermute | solution.py:20
  723.6 12.0 %copy-start.11 = (bf16[1,96,96,128]{2,1,3,0:T(8,128)(2,1)S(1)}, bf16[1,96,96,128]{2,1,3,0:T(8,128)(2,1)}, u32[]{:S(2)}) copy-start(bf16[1,96,96,128]{2,1,3,0:T(8,128)(2,1)} %copy.63) | copy-start | bytes 7077892
  737.3 1.9 copy-start.3
  739.1 1.9 copy-start.31
  739.1 2.2 copy-start.37
  943.8 11.3 %all-to-all-start.1 = ((bf16[16,96,128]{2,1,0:T(8,128)(2,1)}), bf16[16,96,128]{2,1,0:T(8,128)(2,1)S(1)}, u32[]{:S(2)}, u32[]{:S(2)}) async-start(bf16[16,96,128]{2,1,0:T(8,128)(2,1)} %copy.55), calls=%async_computation.1 | async-start | bytes 786432 | tf_op jit(solution)/shard_map/all_to_all | solution.py:84
  (11 other events, 20.8 us)
where the time goes:
time: 967 us; the launch traced here: 957 us
  blocking collectives  704 us (73%)
  local copies, waits for them, and re-layouts  69 us (7%)
  matrix products  64.5 us (7%)
  waiting for transfers between devices  64.4 us (7%)
  starting transfers between devices  29.1 us (3%)
  other arithmetic  23.9 us (2%)
    psum x4, blocking collectives, shards(): alpha = lax.psum(inner(image_out, residual), ('ta', 'gz'))[:, None, None]  256 us
    psum x4, blocking collectives, shards(): squared = lax.psum(inner(image_out, image_out), ('ta', 'gz'))  254 us
    psum x3, blocking collectives, shards(): lax.psum(jnp.stack([inner(earlier, image) for earlier in images]), ('ta',...  194 us
    dot_general x32, matrix products, hop_term(): jnp.einsum('ijs,rjs->ris', hop_links[number], shifted.reshape(count, NC,...  57.5 us
    unnamed x93, local copies, waits for them, and re-layouts  51.8 us
    ppermute x8, waiting for transfers between devices, padded_2(): lax.ppermute(lax.slice_in_dim(block, block.shape[dim] - width, None, axis...  34.8 us
    ppermute x8, waiting for transfers between devices, padded_2(): lax.ppermute(lax.slice_in_dim(block, 0, width, axis=dim), axis, backward)  23 us
  transfers between devices with their start and end apart: 18, of which 16 were waited for; matrix products, arithmetic and copies ran while one was open for 8% of the time, Pallas kernels for 0%

commit v1 on v0

v1 whole, which is shorter than its diff:
```python
import functools

import jax
import jax.numpy as jnp
from jax import lax
from jax.experimental import pallas as pl
from jax.experimental.pallas import tpu as pltpu
from jax.sharding import PartitionSpec as P

MESH = pl.DeviceIdType.MESH
NC = 96
NRHS = 16
ITERS = 4
LOC = 128
GROUPS = 16
SLOTS = 6
CHUNK = 8
F32 = jnp.float32
BF16 = jnp.bfloat16


def lanes(rows=8):
    return lax.broadcasted_iota(jnp.int32, (rows, 128), 1)


def swap_blocks(xs):
    lane = lanes(xs[0].shape[0])
    for b in (1, 2, 4, 8):
        shift = 8 * b
        high = (lane & shift) != 0
        new = list(xs)
        for r in range(16):
            if r & b == 0:
                low_x, high_x = xs[r], xs[r | b]
                new[r] = jnp.where(high, pltpu.roll(high_x, shift, 1), low_x)
                new[r | b] = jnp.where(high, high_x, pltpu.roll(low_x, 128 - shift, 1))
        xs = new
    return xs


def sum_sites(x):
    lane = lanes(x.shape[0])
    for shift in (1, 2, 4):
        other = jnp.where((lane & shift) == 0, pltpu.roll(x, 128 - shift, 1), pltpu.roll(x, shift, 1))
        x = x + other
    return x


def block_diagonal(first, second):
    rows = first.shape[0]
    zeros = jnp.zeros((128, 128), BF16)
    parts = []
    for k in range(rows // 128):
        span = slice(128 * k, 128 * k + 128)
        parts.append(jnp.concatenate([first[span], zeros], axis=1))
        parts.append(jnp.concatenate([zeros, second[span]], axis=1))
    return jnp.concatenate(parts, axis=0)


def kernel(
    n_ta, n_gz,
    restricted, mass, clover, hops,
    sol_out, res_out,
    links, matrix, perm, stage_in, field_in, ext, shifted, mass_f, res, img, acc,
    part1, part2, back_out, back_in,
    link_sem, in_send, in_recv, halo_send, halo_recv, s1_send, s1_recv, s2_send, s2_recv, out_send, out_recv,
):
    ta = lax.axis_index("ta")
    gz = lax.axis_index("gz")
    per = NRHS // n_gz

    def link_copies(c, slot):
        rows = pl.ds(c * CHUNK, CHUNK)
        copies = [pltpu.make_async_copy(clover.at[rows], links.at[slot, :, 0], link_sem.at[slot, 0])]
        for d in range(8):
            copies.append(
                pltpu.make_async_copy(hops.at[d, rows], links.at[slot, :, d + 1], link_sem.at[slot, d + 1])
            )
        return copies

    for c in range(SLOTS):
        for copy in link_copies(c, c):
            copy.start()

    barrier = pltpu.get_barrier_semaphore()
    for o in range(1, n_gz):
        pl.semaphore_signal(barrier, inc=1, device_id=(ta, (gz + o) % n_gz), device_id_type=MESH)
    for o in range(1, n_ta):
        pl.semaphore_signal(barrier, inc=1, device_id=((ta + o) % n_ta, gz), device_id_type=MESH)

    for b in range(n_gz):
        stage_in[b] = restricted[:, :, 128 * b : 128 * b + 128].astype(BF16)
    rows_i = lax.broadcasted_iota(jnp.int32, (256, 256), 0)
    cols_i = lax.broadcasted_iota(jnp.int32, (256, 256), 1)
    wanted = ((rows_i // 8) % 2) * 128 + (rows_i // 16) * 8 + rows_i % 8
    perm[...] = jnp.where(cols_i == wanted, 1.0, 0.0).astype(BF16)

    pl.semaphore_wait(barrier, n_gz - 1 + n_ta - 1)

    def in_copy(o):
        to = (gz + o) % n_gz
        return pltpu.make_async_remote_copy(
            src_ref=stage_in.at[to],
            dst_ref=field_in.at[pl.ds(gz * per, per)],
            send_sem=in_send.at[o],
            recv_sem=in_recv.at[o],
            device_id=(ta, to),
            device_id_type=MESH,
        )

    for o in range(1, n_gz):
        in_copy(o).start()
    field_in[pl.ds(gz * per, per)] = stage_in[gz]

    def mass_step(c, carry):
        rows = pl.ds(pl.multiple_of(c * 8, 8), 8)
        m = mass[rows, :]
        spread = swap_blocks([m] * 16)
        for g in range(GROUPS):
            mass_f[g, rows, :] = spread[g]
        return carry

    lax.fori_loop(0, NC // 8, mass_step, 0)

    def prepare(c, carry):
        slot = c % SLOTS
        for copy in link_copies(c, slot):
            copy.wait()
        pad = jnp.zeros((32, 128), BF16)
        for pair in range(CHUNK // 2):
            sides = []
            for i2 in range(2):
                block = links[slot, 2 * pair + i2]
                head = block[:5].reshape(5 * NC, 128)
                tail = block[5:].reshape(4 * NC, 128)
                sides.append(jnp.concatenate([head, pad, tail], axis=0))
            both = jnp.concatenate(sides, axis=1)
            turned = lax.dot_general(
                perm[...], both, (((1,), (1,)), ((), ())), preferred_element_type=F32
            ).astype(BF16)
            rows = pl.ds(pl.multiple_of((c * (CHUNK // 2) + pair) * 16, 16), 16)
            for g in range(GROUPS):
                for k in range(7):
                    start = k * 256 + (g % 2) * 128
                    matrix[g // 2, rows, start : start + 128] = turned[
                        16 * g : 16 * g + 16, 128 * k : 128 * k + 128
                    ]

        @pl.when(c + SLOTS < NC // CHUNK)
        def _():
            for copy in link_copies(c + SLOTS, slot):
                copy.start()

        return carry

    def fill(tz, first, second):
        t, z = tz // 4, tz % 4
        lane = lanes(NC)
        low_x = (lane & 4) == 0
        y = lane & 3
        swaps = []
        for half, v in enumerate((first, second)):
            ext[t + 1, z + 1, half] = v.astype(BF16)
            up = jnp.where(y < 3, pltpu.roll(v, 127, 1), pltpu.roll(v, 3, 1))
            down = jnp.where(y > 0, pltpu.roll(v, 1, 1), pltpu.roll(v, 125, 1))
            shifted[2, tz * 2 + half] = up.astype(BF16)
            shifted[3, tz * 2 + half] = down.astype(BF16)
            swaps.append(jnp.where(low_x, pltpu.roll(v, 124, 1), pltpu.roll(v, 4, 1)))
        for half in range(2):
            own, other = swaps[half], swaps[1 - half]
            shifted[0, tz * 2 + half] = jnp.where(low_x, own, other).astype(BF16)
            shifted[1, tz * 2 + half] = jnp.where(low_x, other, own).astype(BF16)

    def halo_copies():
        ta_up, ta_down = (ta + 1) % n_ta, (ta + n_ta - 1) % n_ta
        gz_up, gz_down = (gz + 1) % n_gz, (gz + n_gz - 1) % n_gz
        moves = (
            (ext.at[1, 1:5], ext.at[3, 1:5], (ta_down, gz)),
            (ext.at[2, 1:5], ext.at[0, 1:5], (ta_up, gz)),
            (ext.at[1:3, 1], ext.at[1:3, 5], (ta, gz_down)),
            (ext.at[1:3, 4], ext.at[1:3, 0], (ta, gz_up)),
        )
        return [
            pltpu.make_async_remote_copy(
                src_ref=src, dst_ref=dst, send_sem=halo_send.at[n], recv_sem=halo_recv.at[n],
                device_id=to, device_id_type=MESH,
            )
            for n, (src, dst, to) in enumerate(moves)
        ]

    def near_products(tz, carry):
        t, z = tz // 4, tz % 4
        pad = jnp.zeros((32, 128), BF16)
        sides = []
        for half in range(2):
            g = tz * 2 + half
            pieces = [ext[t + 1, z + 1, half]] + [shifted[d, g] for d in range(4)] + [pad]
            sides.append(jnp.concatenate(pieces, axis=0))
        out = jnp.dot(matrix[tz, :, :1024], block_diagonal(*sides), preferred_element_type=F32)
        acc[tz, 0] = out[:, :128]
        acc[tz, 1] = out[:, 128:]
        return carry

    def far_products(number, tz, carry):
        t, z = tz // 4, tz % 4
        sides = []
        for half in range(2):
            pieces = [
                ext[t + 1, z + 2, half], ext[t + 1, z, half], ext[t + 2, z + 1, half], ext[t, z + 1, half]
            ]
            sides.append(jnp.concatenate(pieces, axis=0))
        out = jnp.dot(matrix[tz, :, 1024:], block_diagonal(*sides), preferred_element_type=F32)
        acc[tz, 0] += out[:, :128]
        acc[tz, 1] += out[:, 128:]
        site = lanes() & 7
        carry = list(carry)
        for half in range(2):
            g = tz * 2 + half
            for ib in range(NC // 8):
                total = acc[tz, half, pl.ds(ib * 64, 8, stride=8), :]
                for s in range(1, 8):
                    total = jnp.where(site == s, acc[tz, half, pl.ds(ib * 64 + s, 8, stride=8), :], total)
                rows = pl.ds(ib * 8, 8)
                r = res[number, g, rows, :]
                q = total + mass_f[g, rows, :] * r
                img[number, g, rows, :] = q
                for j in range(number):
                    carry[j] = carry[j] + img[j, g, rows, :] * q
                carry[number] = carry[number] + q * q
                carry[number + 1] = carry[number + 1] + q * r
        return tuple(carry)

    def total_over_devices(number, value):
        part1[number, gz] = value
        copies = []
        for o in range(1, n_gz):
            copies.append(
                pltpu.make_async_remote_copy(
                    src_ref=part1.at[number, gz], dst_ref=part1.at[number, gz],
                    send_sem=s1_send.at[number, o], recv_sem=s1_recv.at[number, o],
                    device_id=(ta, (gz + o) % n_gz), device_id_type=MESH,
                )
            )
        for copy in copies:
            copy.start()
        for copy in copies:
            copy.wait_recv()
        value = part1[number, 0]
        for o in range(1, n_gz):
            value = value + part1[number, o]
        for copy in copies:
            copy.wait_send()
        part2[number, ta] = value
        copies = []
        for o in range(1, n_ta):
            copies.append(
                pltpu.make_async_remote_copy(
                    src_ref=part2.at[number, ta], dst_ref=part2.at[number, ta],
                    send_sem=s2_send.at[number, o], recv_sem=s2_recv.at[number, o],
                    device_id=((ta + o) % n_ta, gz), device_id_type=MESH,
                )
            )
        for copy in copies:
            copy.start()
        for copy in copies:
            copy.wait_recv()
        value = part2[number, 0]
        for o in range(1, n_ta):
            value = value + part2[number, o]
        for copy in copies:
            copy.wait_send()
        return sum_sites(value)

    lax.fori_loop(0, 4, prepare, 0)
    for o in range(1, n_gz):
        in_copy(o).wait_recv()

    def arrange(c, carry):
        rows = pl.ds(pl.multiple_of(c * 16, 16), 16)
        xs = swap_blocks([field_in[r, rows, :].astype(F32) for r in range(NRHS)])
        for g in range(GROUPS):
            res[0, g, rows, :] = xs[g]
        return carry

    lax.fori_loop(0, NC // 16, arrange, 0)

    def first_fill(tz, carry):
        fill(tz, res[0, tz * 2], res[0, tz * 2 + 1])
        return carry

    lax.fori_loop(0, 8, first_fill, 0)
    for copy in halo_copies():
        copy.start()
    lax.fori_loop(4, NC // CHUNK, prepare, 0)
    for o in range(1, n_gz):
        in_copy(o).wait_send()

    gram = {}
    with_res = []
    coef = []
    sol_coef = []
    for number in range(ITERS):
        if number > 0:
            for copy in halo_copies():
                copy.start()
        lax.fori_loop(0, 8, near_products, 0)
        for copy in halo_copies():
            copy.wait()
        zero = jnp.zeros((8, 128), F32)
        sums = lax.fori_loop(0, 8, functools.partial(far_products, number), (zero,) * (number + 2))
        rows = [jnp.sum(x, axis=0, keepdims=True) for x in sums]
        value = jnp.concatenate(rows + [jnp.zeros((8 - len(rows), 128), F32)], axis=0)
        value = total_over_devices(number, value)
        beta = [value[j : j + 1] for j in range(number)]
        squared = value[number : number + 1]
        along = value[number + 1 : number + 2]
        cross = []
        for j in range(number):
            proj = beta[0] * gram[0, j]
            for l in range(1, number):
                proj = proj + beta[l] * gram[l, j]
            cross.append(proj)
        for j in range(number):
            squared = squared - beta[j] * (2.0 * beta[j] - cross[j])
            along = along - beta[j] * with_res[j]
        squared = jnp.maximum(squared, 0.0)
        inverse = 1.0 / jnp.sqrt(squared + 1e-06)
        alpha = along * inverse
        for j in range(number):
            gram[number, j] = gram[j, number] = (beta[j] - cross[j]) * inverse
        gram[number, number] = squared * inverse * inverse
        with_res = [w - alpha * gram[j, number] for j, w in enumerate(with_res)]
        with_res.append(alpha - alpha * gram[number, number])
        mine = []
        for m in range(number):
            total = beta[m] * coef[m][m]
            for j in range(m + 1, number):
                total = total + beta[j] * coef[j][m]
            mine.append(-total * inverse)
        mine.append(inverse)
        coef.append(mine)
        sol_coef = [c + alpha * mine[m] for m, c in enumerate(sol_coef)] + [alpha * inverse]

        def update(tz, carry):
            fresh = []
            for half in range(2):
                g = tz * 2 + half
                q = img[number, g]
                for j in range(number):
                    q = q - beta[j] * img[j, g]
                q = q * inverse
                if number < ITERS - 1:
                    img[number, g] = q
                r = res[number, g] - alpha * q
                res[number + 1, g] = r
                fresh.append(r)
            if number < ITERS - 1:
                fill(tz, *fresh)
            return carry

        if number < ITERS - 1:
            lax.fori_loop(0, 8, update, 0)

    def finish(c, carry):
        rows = pl.ds(pl.multiple_of(c * 16, 16), 16)
        xs = []
        for g in range(GROUPS):
            x = sol_coef[0] * res[0, g, rows, :]
            for m in range(1, ITERS):
                x = x + sol_coef[m] * res[m, g, rows, :]
            xs.append(x)
        xs = swap_blocks(xs)
        for r in range(NRHS):
            back_out[r, rows, :] = xs[r].astype(BF16)
        return carry

    lax.fori_loop(0, NC // 16, finish, 0)

    def out_copy(o):
        to = (gz + o) % n_gz
        return pltpu.make_async_remote_copy(
            src_ref=back_out.at[pl.ds(to * per, per)],
            dst_ref=back_in.at[gz],
            send_sem=out_send.at[o],
            recv_sem=out_recv.at[o],
            device_id=(ta, to),
            device_id_type=MESH,
        )

    for o in range(1, n_gz):
        out_copy(o).start()
    back_in[gz] = back_out[pl.ds(gz * per, per)]

    def last_residual(c, carry):
        rows = pl.ds(pl.multiple_of(c * 8, 8), 8)
        xs = []
        for g in range(GROUPS):
            q = img[ITERS - 1, g, rows, :]
            for j in range(ITERS - 1):
                q = q - beta[j] * img[j, g, rows, :]
            xs.append(res[ITERS - 1, g, rows, :] - alpha * (q * inverse))
        xs = swap_blocks(xs)
        for r in range(NRHS):
            res_out[r, rows, :] = xs[r]
        return carry

    lax.fori_loop(0, NC // 8, last_residual, 0)
    for o in range(1, n_gz):
        out_copy(o).wait()
    for b in range(n_gz):
        sol_out[:, :, 128 * b : 128 * b + 128] = back_in[b].astype(F32)


def solution(mesh):
    n_ta, n_gz = mesh.shape["ta"], mesh.shape["gz"]
    per = NRHS // n_gz

    def step(restricted, mass_terms, clover_blocks, hop_links):
        vmem = pl.BlockSpec(memory_space=pltpu.VMEM)
        hbm = pl.BlockSpec(memory_space=pl.ANY)
        dma = pltpu.SemaphoreType.DMA
        return pl.pallas_call(
            functools.partial(kernel, n_ta, n_gz),
            out_shape=(
                jax.ShapeDtypeStruct((per, NC, LOC * n_gz), F32),
                jax.ShapeDtypeStruct((NRHS, NC, LOC), F32),
            ),
            in_specs=[vmem, vmem, hbm, hbm],
            out_specs=(vmem, vmem),
            scratch_shapes=[
                pltpu.VMEM((SLOTS, CHUNK, 9, NC, 128), BF16),
                pltpu.VMEM((8, 8 * NC, 7 * 256), BF16),
                pltpu.VMEM((256, 256), BF16),
                pltpu.VMEM((n_gz, per, NC, 128), BF16),
                pltpu.VMEM((NRHS, NC, 128), BF16),
                pltpu.VMEM((4, 6, 2, NC, 128), BF16),
                pltpu.VMEM((4, GROUPS, NC, 128), BF16),
                pltpu.VMEM((GROUPS, NC, 128), F32),
                pltpu.VMEM((ITERS, GROUPS, NC, 128), F32),
                pltpu.VMEM((ITERS, GROUPS, NC, 128), F32),
                pltpu.VMEM((8, 2, 8 * NC, 128), F32),
                pltpu.VMEM((ITERS, n_gz, 8, 128), F32),
                pltpu.VMEM((ITERS, n_ta, 8, 128), F32),
                pltpu.VMEM((NRHS, NC, 128), BF16),
                pltpu.VMEM((n_gz, per, NC, 128), BF16),
                dma((SLOTS, 9)),
                dma((n_gz,)),
                dma((n_gz,)),
                dma((4,)),
                dma((4,)),
                dma((ITERS, n_gz)),
                dma((ITERS, n_gz)),
                dma((ITERS, n_ta)),
                dma((ITERS, n_ta)),
                dma((n_gz,)),
                dma((n_gz,)),
            ],
            compiler_params=pltpu.CompilerParams(
                collective_id=0, has_side_effects=True, vmem_limit_bytes=60 * 1024 * 1024
            ),
        )(restricted, mass_terms, clover_blocks, hop_links)

    return jax.shard_map(
        step,
        mesh=mesh,
        in_specs=(
            P("gz", None, "ta"),
            P(None, ("ta", "gz")),
            P(None, None, ("ta", "gz")),
            P(None, None, None, ("ta", "gz")),
        ),
        out_specs=(P("gz", None, "ta"), P(None, None, ("ta", "gz"))),
        check_vma=False,
    )
```

time: 967 us -> 139 us (0.14); the launches traced: 957 us -> 139 us
  blocking collectives: 704 us -> 0 us
  Pallas kernels: 0 us -> 134 us
  local copies, waits for them, and re-layouts: 69 us -> 4.16 us
  matrix products: 64.5 us -> 0 us
  waiting for transfers between devices: 64.4 us -> 0 us
  starting transfers between devices: 29.1 us -> 0 us
  other arithmetic: 23.9 us -> 0 us
    psum x11 -> x0, blocking collectives: 704 us -> none  [the longest x4 256 us: shards(): alpha = lax.psum(inner(image_out, residual), ('ta', 'gz'))[:, None, None]]
    pallas_call x0 -> x1, Pallas kernels: none -> 134 us  [step(): pl.pallas_call(functools.partial(kernel, n_ta, n_gz), out_shape=(jax.Shap...]
    dot_general x36 -> x0, matrix products: 64.5 us -> none  [the longest x32 57.5 us: hop_term(): jnp.einsum('ijs,rjs->ris', hop_links[number], shifted.reshape(count, NC,...]
    ppermute x16 -> x0, waiting for transfers between devices: 57.8 us -> none  [the longest x8 34.8 us: padded_2(): lax.ppermute(lax.slice_in_dim(block, block.shape[dim] - width, None, axis...]
    unnamed x93 -> x2, local copies, waits for them, and re-layouts: 51.8 us -> 4.16 us
    ppermute x16 -> x0, starting transfers between devices: 18.8 us -> none  [the longest x8 10.6 us: padded_2(): lax.ppermute(lax.slice_in_dim(block, block.shape[dim] - width, None, axis...]
    slice x21 -> x0, local copies, waits for them, and re-layouts: 14.6 us -> none  [the longest x1 13.1 us: hop_term(): hop_links[number]]
    reduce_sum x7 -> x0, other arithmetic: 12.1 us -> none  [inner(): return jnp.sum(left * right, axis=(1, 2))]
  transfers between devices with their start and end apart: 18 -> 0, of which waited for: 16 -> 0; matrix products, arithmetic and copies ran while one was open for 8% -> 0% of each run, Pallas kernels for 0% -> 0%
where the time goes in v1:
time: 139 us
  Pallas kernels  134 us (96%)
  local copies, waits for them, and re-layouts  4.16 us (3%)
    pallas_call x1, Pallas kernels, step(): pl.pallas_call(functools.partial(kernel, n_ta, n_gz), out_shape=(jax.Shap...  134 us
    unnamed x2, local copies, waits for them, and re-layouts  4.16 us

profile of v1, /device:TPU:1, one launch (start us, length us, event | category | flops | bytes accessed | tf_op | source)
XLA Modules:
  0.0 138.7 jit_solution(17606067450763077972)
XLA Ops:
  0.6 133.9 %shard_map.59 = (f32[2,96,1024]{2,1,0:T(8,128)}, f32[16,96,128]{2,1,0:T(8,128)}) custom-call(f32[2,96,1024]{2,1,0:T(8,128)} %restricted.1, f32[96,128]{1,0:T(8,128)} %mass.1, bf16[96,96,128]{2,1,0:T(8,128)(2,1)} %clover.1, bf16[8,96,96,128]{3,2,1,0:T(8,128)(2,1)} %hops.1), custom_call_target="tpu_custom_call" | custom-call | tf_op jit(solution)/shard_map/pallas_call | solution.py:422
  134.5 2.1 %copy.8 = f32[2,96,1024]{2,1,0:T(8,128)} copy(f32[2,96,1024]{2,1,0:T(8,128)} %get-tuple-element.4) | data formatting | bytes 1572864
  136.6 2.1 %copy.9 = f32[16,96,128]{2,1,0:T(8,128)} copy(f32[16,96,128]{2,1,0:T(8,128)} %get-tuple-element.5) | data formatting | bytes 1572864

commit v2 on v1

v2 whole, which is shorter than its diff:
```python
import functools

import jax
import jax.numpy as jnp
from jax import lax
from jax.experimental import pallas as pl
from jax.experimental.pallas import tpu as pltpu
from jax.sharding import PartitionSpec as P

MESH = pl.DeviceIdType.MESH
NC = 96
NRHS = 16
ITERS = 4
LOC = 128
GROUPS = 16
SLOTS = 6
CHUNK = 8
SHIFT = 3.0
F32 = jnp.float32
BF16 = jnp.bfloat16


def lanes(rows=8):
    return lax.broadcasted_iota(jnp.int32, (rows, 128), 1)


def swap_blocks(xs):
    lane = lanes(xs[0].shape[0])
    for b in (1, 2, 4, 8):
        shift = 8 * b
        high = (lane & shift) != 0
        new = list(xs)
        for r in range(16):
            if r & b == 0:
                low_x, high_x = xs[r], xs[r | b]
                new[r] = jnp.where(high, pltpu.roll(high_x, shift, 1), low_x)
                new[r | b] = jnp.where(high, high_x, pltpu.roll(low_x, 128 - shift, 1))
        xs = new
    return xs


def sum_sites(x):
    lane = lanes(x.shape[0])
    for shift in (1, 2, 4):
        other = jnp.where((lane & shift) == 0, pltpu.roll(x, 128 - shift, 1), pltpu.roll(x, shift, 1))
        x = x + other
    return x


def block_diagonal(first, second):
    rows = first.shape[0]
    zeros = jnp.zeros((128, 128), BF16)
    parts = []
    for k in range(rows // 128):
        span = slice(128 * k, 128 * k + 128)
        parts.append(jnp.concatenate([first[span], zeros], axis=1))
        parts.append(jnp.concatenate([zeros, second[span]], axis=1))
    return jnp.concatenate(parts, axis=0)


def kernel(
    n_ta, n_gz,
    restricted, mass, clover, hops,
    sol_out, res_out,
    links, matrix, perm, stage_in, field_in, own, halo_t, halo_z, ext, mass_f, basis, near, acc,
    part1, part2, back_out, back_in,
    link_sem, in_send, in_recv, t_send, t_recv, z_send, z_recv, s1_send, s1_recv, s2_send, s2_recv, out_send, out_recv,
):
    ta = lax.axis_index("ta")
    gz = lax.axis_index("gz")
    per = NRHS // n_gz
    ta_up, ta_down = (ta + 1) % n_ta, (ta + n_ta - 1) % n_ta
    gz_up, gz_down = (gz + 1) % n_gz, (gz + n_gz - 1) % n_gz
    ta_low, gz_low = min(4, n_ta), min(2, n_gz)
    ta_high, gz_high = n_ta // ta_low, n_gz // gz_low
    th, tl, gh, gl = ta // ta_low, ta % ta_low, gz // gz_low, gz % gz_low
    place1 = tl * gz_low + gl
    place2 = th * gz_high + gh
    peers1 = [
        (th * ta_low + (tl + a) % ta_low, gh * gz_low + (gl + b) % gz_low)
        for a in range(ta_low) for b in range(gz_low) if a or b
    ]
    peers2 = [
        (((th + a) % ta_high) * ta_low + tl, ((gh + b) % gz_high) * gz_low + gl)
        for a in range(ta_high) for b in range(gz_high) if a or b
    ]

    def link_copies(c, slot):
        rows = pl.ds(c * CHUNK, CHUNK)
        copies = [pltpu.make_async_copy(clover.at[rows], links.at[slot, :, 0], link_sem.at[slot, 0])]
        for d in range(8):
            copies.append(
                pltpu.make_async_copy(hops.at[d, rows], links.at[slot, :, d + 1], link_sem.at[slot, d + 1])
            )
        return copies

    barrier = pltpu.get_barrier_semaphore()
    greet = [(ta, (gz + o) % n_gz) for o in range(1, n_gz)] + peers1 + peers2 + [(ta_up, gz), (ta_down, gz)]
    for to in greet:
        pl.semaphore_signal(barrier, inc=1, device_id=to, device_id_type=MESH)

    for c in range(SLOTS):
        for copy in link_copies(c, c):
            copy.start()

    for b in range(n_gz):
        stage_in[b] = restricted[:, :, 128 * b : 128 * b + 128].astype(BF16)
    rows_i = lax.broadcasted_iota(jnp.int32, (256, 256), 0)
    cols_i = lax.broadcasted_iota(jnp.int32, (256, 256), 1)
    wanted = ((rows_i // 8) % 2) * 128 + (rows_i // 16) * 8 + rows_i % 8
    perm[...] = jnp.where(cols_i == wanted, 1.0, 0.0).astype(BF16)

    def mass_step(c, carry):
        rows = pl.ds(pl.multiple_of(c * 16, 16), 16)
        m = mass[rows, :] - SHIFT
        spread = swap_blocks([m] * 16)
        for g in range(GROUPS):
            mass_f[g, rows, :] = spread[g]
        return carry

    lax.fori_loop(0, NC // 16, mass_step, 0, unroll=2)

    pl.semaphore_wait(barrier, len(greet))

    def in_copy(o):
        to = (gz + o) % n_gz
        return pltpu.make_async_remote_copy(
            src_ref=stage_in.at[to],
            dst_ref=field_in.at[pl.ds(gz * per, per)],
            send_sem=in_send.at[o],
            recv_sem=in_recv.at[o],
            device_id=(ta, to),
            device_id_type=MESH,
        )

    for o in range(1, n_gz):
        in_copy(o).start()
    field_in[pl.ds(gz * per, per)] = stage_in[gz]

    def prepare(c, carry):
        slot = c % SLOTS
        for copy in link_copies(c, slot):
            copy.wait()
        pad = jnp.zeros((32, 128), BF16)
        for pair in range(CHUNK // 2):
            sides = []
            for i2 in range(2):
                block = links[slot, 2 * pair + i2]
                front = block[:5].reshape(5 * NC, 128)
                tail = block[5:].reshape(4 * NC, 128)
                sides.append(jnp.concatenate([front, pad, tail], axis=0))
            both = jnp.concatenate(sides, axis=1)
            turned = lax.dot_general(
                perm[...], both, (((1,), (1,)), ((), ())), preferred_element_type=F32
            ).astype(BF16)
            rows = pl.ds(pl.multiple_of((c * (CHUNK // 2) + pair) * 16, 16), 16)
            for g in range(GROUPS):
                for k in range(7):
                    start = k * 256 + (g % 2) * 128
                    matrix[g // 2, rows, start : start + 128] = turned[
                        16 * g : 16 * g + 16, 128 * k : 128 * k + 128
                    ]

        @pl.when(c + SLOTS < NC // CHUNK)
        def _():
            for copy in link_copies(c + SLOTS, slot):
                copy.start()

        return carry

    def t_copy(m, t, z):
        side = 1 - t
        return pltpu.make_async_remote_copy(
            src_ref=own.at[m, t, z], dst_ref=halo_t.at[m, side, z],
            send_sem=t_send.at[m, side, z], recv_sem=t_recv.at[m, side, z],
            device_id=(ta_up if t else ta_down, gz), device_id_type=MESH,
        )

    def z_copy(m, side):
        return pltpu.make_async_remote_copy(
            src_ref=own.at[m, :, 0 if side else 3], dst_ref=halo_z.at[m, side],
            send_sem=z_send.at[m, side], recv_sem=z_recv.at[m, side],
            device_id=(ta, gz_down if side else gz_up), device_id_type=MESH,
        )

    def send_halo(m, z):
        t_copy(m, 0, z).start()
        t_copy(m, 1, z).start()

        @pl.when(z == 0)
        def _():
            z_copy(m, 1).start()

        @pl.when(z == 3)
        def _():
            z_copy(m, 0).start()

    def chosen(t, half):
        site = lanes() & 7
        parts = []
        for ib in range(NC // 8):
            total = acc[t, half, pl.ds(ib * 64, 8, stride=8), :]
            for s in range(1, 8):
                total = jnp.where(site == s, acc[t, half, pl.ds(ib * 64 + s, 8, stride=8), :], total)
            parts.append(total)
        return jnp.concatenate(parts, axis=0)

    def near_products(k, mix, i, carry):
        z = lax.rem(3 * i, 4)
        lane = lanes(NC)
        low_x = (lane & 4) == 0
        y = lane & 3
        pad = jnp.zeros((32, 128), BF16)
        for t in range(2):
            vs, swaps, sides = [], [], []
            for half in range(2):
                g = (t * 4 + z) * 2 + half
                if k < 2:
                    v = basis[k, g]
                else:
                    v = mix[0] * basis[1, g]
                    for m in range(1, k):
                        v = v + mix[m] * basis[m + 1, g]
                vs.append(v)
                swaps.append(jnp.where(low_x, pltpu.roll(v, 124, 1), pltpu.roll(v, 4, 1)))
            for half in range(2):
                v, here, there = vs[half], swaps[half], swaps[1 - half]
                center = v.astype(BF16)
                ext[t + 1, z + 1, half] = center
                pieces = [
                    center,
                    jnp.where(low_x, here, there).astype(BF16),
                    jnp.where(low_x, there, here).astype(BF16),
                    jnp.where(y < 3, pltpu.roll(v, 127, 1), pltpu.roll(v, 3, 1)).astype(BF16),
                    jnp.where(y > 0, pltpu.roll(v, 1, 1), pltpu.roll(v, 125, 1)).astype(BF16),
                    pad,
                ]
                sides.append(jnp.concatenate(pieces, axis=0))
            out = jnp.dot(matrix[t * 4 + z, :, :1024], block_diagonal(*sides), preferred_element_type=F32)
            acc[t, 0] = out[:, :128]
            acc[t, 1] = out[:, 128:]
            for half in range(2):
                g = (t * 4 + z) * 2 + half
                near[g] = chosen(t, half) + mass_f[g] * vs[half]
        return carry

    def far_products(k, mix, i, carry):
        z = lax.rem(3 * i, 4)

        def mixed(ref, *at):
            if k < 2:
                return ref[(k, *at)]
            v = mix[0] * ref[(1, *at)].astype(F32)
            for m in range(1, k):
                v = v + mix[m] * ref[(m + 1, *at)].astype(F32)
            return v.astype(BF16)

        for t in range(2):
            t_copy(k, 1 - t, z).wait_recv()
            for half in range(2):
                ext[3 * t, z + 1, half] = mixed(halo_t, t, z, half)

        for edge, side in ((0, 0), (3, 1)):

            @pl.when(z == edge)
            def _():
                z_copy(k, side).wait_recv()
                for t in range(2):
                    for half in range(2):
                        ext[t + 1, 5 * side, half] = mixed(halo_z, side, t, half)

        carry = list(carry)
        for t in range(2):
            sides = []
            for half in range(2):
                pieces = [
                    ext[t + 1, z + 2, half], ext[t + 1, z, half], ext[t + 2, z + 1, half], ext[t, z + 1, half]
                ]
                sides.append(jnp.concatenate(pieces, axis=0))
            out = jnp.dot(matrix[t * 4 + z, :, 1024:], block_diagonal(*sides), preferred_element_type=F32)
            acc[t, 0] = out[:, :128]
            acc[t, 1] = out[:, 128:]
            for half in range(2):
                g = (t * 4 + z) * 2 + half
                new = near[g] + chosen(t, half)
                basis[k + 1, g] = new
                if k < ITERS - 1:
                    own[k + 1, t, z, half] = new.astype(BF16)
                others = [basis[j, g] for j in range(k + 1)]
                products = [other * new for other in others] + [new * new]
                if k == 0:
                    products.append(others[0] * others[0])
                for j, product in enumerate(products):
                    carry[j] = carry[j] + jnp.sum(product.reshape(NC // 8, 8, 128), axis=0)
        if k < ITERS - 1:
            send_halo(k + 1, z)
        return tuple(carry)

    def share(number, stage):
        buf, place, peers, send, recv = (
            (part1, place1, peers1, s1_send, s1_recv), (part2, place2, peers2, s2_send, s2_recv)
        )[stage]
        return [
            pltpu.make_async_remote_copy(
                src_ref=buf.at[number, place], dst_ref=buf.at[number, place],
                send_sem=send.at[number, n], recv_sem=recv.at[number, n],
                device_id=to, device_id_type=MESH,
            )
            for n, to in enumerate(peers)
        ]

    def sum_start(number, value):
        part1[number, place1] = value
        for copy in share(number, 0):
            copy.start()

    def sum_middle(number):
        for copy in share(number, 0):
            copy.wait_recv()
        value = part1[number, 0]
        for n in range(1, ta_low * gz_low):
            value = value + part1[number, n]
        part2[number, place2] = value
        for copy in share(number, 1):
            copy.start()

    def sum_end(number):
        for copy in share(number, 1):
            copy.wait_recv()
        value = part2[number, 0]
        for n in range(1, ta_high * gz_high):
            value = value + part2[number, n]
        return sum_sites(value)

    lax.fori_loop(0, 6, prepare, 0)
    for o in range(1, n_gz):
        in_copy(o).wait_recv()

    def arrange(c, carry):
        rows = pl.ds(pl.multiple_of(c * 16, 16), 16)
        xs = swap_blocks([field_in[r, rows, :].astype(F32) for r in range(NRHS)])
        for g in range(GROUPS):
            basis[0, g, rows, :] = xs[g]
            own[0, g // 8, (g // 2) % 4, g % 2, rows, :] = xs[g].astype(BF16)
        return carry

    lax.fori_loop(0, NC // 16, arrange, 0, unroll=2)
    for z in range(4):
        t_copy(0, 0, z).start()
        t_copy(0, 1, z).start()
    z_copy(0, 1).start()
    z_copy(0, 0).start()
    lax.fori_loop(6, NC // CHUNK, prepare, 0)

    size = ITERS + 1
    gram = {}

    def unit(m):
        return [1.0 if n == m else None for n in range(size)]

    def add(u, c, w):
        out = []
        for a, b in zip(u, w):
            if b is None:
                out.append(a)
            else:
                out.append(c * b if a is None else a + c * b)
        return out

    def scale(c, w):
        return [None if b is None else c * b for b in w]

    def apply_gram(w):
        out = []
        for m in range(size):
            total = None
            for n in range(size):
                if w[n] is not None and (m, n) in gram:
                    term = w[n] * gram[m, n]
                    total = term if total is None else total + term
            out.append(total)
        return out

    def pair_up(u, gw):
        total = None
        for a, b in zip(u, gw):
            if a is not None and b is not None:
                total = a * b if total is None else total + a * b
        return total

    r, p, x = unit(0), unit(1), [None] * size
    images, searches, image_products = [], [], []
    mix = None

    def iterate(k, r, p, x):
        q = add(p, SHIFT, r)
        gq = apply_gram(q)
        betas = [pair_up(image, gq) for image in images]
        qo, po = q, r
        for beta, image, search in zip(betas, images, searches):
            qo, po = add(qo, -beta, image), add(po, -beta, search)
        gqo = apply_gram(qo)
        inverse = 1.0 / jnp.sqrt(jnp.maximum(pair_up(qo, gqo), 0.0) + 1e-06)
        alpha = pair_up(r, gqo) * inverse
        qo, po = scale(inverse, qo), scale(inverse, po)
        x = add(x, alpha, po)
        if k < ITERS - 1:
            bq = add(unit(k + 2), SHIFT, p)
            for beta, product in zip(betas, image_products):
                bq = add(bq, -beta, product)
            bq = scale(inverse, bq)
            image_products.append(bq)
            p = add(p, -alpha, bq)
        r = add(r, -alpha, qo)
        images.append(qo)
        searches.append(po)
        return r, p, x

    def take_gram(k, value):
        for j in range(k + 2):
            gram[j, k + 1] = gram[k + 1, j] = value[j : j + 1]
        if k == 0:
            gram[0, 0] = value[2:3]
            gram[0, 1] = gram[1, 0] = value[0:1]
            gram[1, 1] = value[1:2]

    for k in range(ITERS):
        lax.fori_loop(0, 4, functools.partial(near_products, k, mix), 0)
        if k > 0:
            sum_middle(k - 1)
        count = k + 2 + (k == 0)
        zero = jnp.zeros((8, 128), F32)
        sums = lax.fori_loop(0, 4, functools.partial(far_products, k, mix), (zero,) * count)
        rows = [jnp.sum(v, axis=0, keepdims=True) for v in sums]
        sum_start(k, jnp.concatenate(rows + [jnp.zeros((8 - count, 128), F32)], axis=0))
        if k > 0:
            take_gram(k - 1, sum_end(k - 1))
            r, p, x = iterate(k - 1, r, p, x)
            mix = p[1 : k + 2]
    sum_middle(ITERS - 1)
    take_gram(ITERS - 1, sum_end(ITERS - 1))
    r, p, x = iterate(ITERS - 1, r, p, x)

    def combine(coefs, g, rows):
        total = None
        for m, c in enumerate(coefs):
            if c is not None:
                term = c * basis[m, g, rows, :]
                total = term if total is None else total + term
        return total

    def finish(c, carry):
        rows = pl.ds(pl.multiple_of(c * 16, 16), 16)
        xs = swap_blocks([combine(x, g, rows) for g in range(GROUPS)])
        for n in range(NRHS):
            back_out[n, rows, :] = xs[n].astype(BF16)
        return carry

    lax.fori_loop(0, NC // 16, finish, 0, unroll=2)

    def out_copy(o):
        to = (gz + o) % n_gz
        return pltpu.make_async_remote_copy(
            src_ref=back_out.at[pl.ds(to * per, per)],
            dst_ref=back_in.at[gz],
            send_sem=out_send.at[o],
            recv_sem=out_recv.at[o],
            device_id=(ta, to),
            device_id_type=MESH,
        )

    for o in range(1, n_gz):
        out_copy(o).start()
    back_in[gz] = back_out[pl.ds(gz * per, per)]

    def last_residual(c, carry):
        rows = pl.ds(pl.multiple_of(c * 16, 16), 16)
        xs = swap_blocks([combine(r, g, rows) for g in range(GROUPS)])
        for n in range(NRHS):
            res_out[n, rows, :] = xs[n]
        return carry

    lax.fori_loop(0, NC // 16, last_residual, 0, unroll=2)

    for o in range(1, n_gz):
        in_copy(o).wait_send()
    for m in range(ITERS):
        for z in range(4):
            t_copy(m, 0, z).wait_send()
            t_copy(m, 1, z).wait_send()
        z_copy(m, 0).wait_send()
        z_copy(m, 1).wait_send()
        for stage in range(2):
            for copy in share(m, stage):
                copy.wait_send()
    for o in range(1, n_gz):
        out_copy(o).wait()
    for b in range(n_gz):
        sol_out[:, :, 128 * b : 128 * b + 128] = back_in[b]


def solution(mesh):
    n_ta, n_gz = mesh.shape["ta"], mesh.shape["gz"]
    per = NRHS // n_gz
    first = min(4, n_ta) * min(2, n_gz)
    second = n_ta * n_gz // first

    def step(restricted, mass_terms, clover_blocks, hop_links):
        vmem = pl.BlockSpec(memory_space=pltpu.VMEM)
        hbm = pl.BlockSpec(memory_space=pl.ANY)
        dma = pltpu.SemaphoreType.DMA
        sol, res = pl.pallas_call(
            functools.partial(kernel, n_ta, n_gz),
            out_shape=(
                jax.ShapeDtypeStruct((per, NC, LOC * n_gz), BF16),
                jax.ShapeDtypeStruct((NRHS, NC, LOC), F32),
            ),
            in_specs=[vmem, vmem, hbm, hbm],
            out_specs=(vmem, vmem),
            scratch_shapes=[
                pltpu.VMEM((SLOTS, CHUNK, 9, NC, 128), BF16),
                pltpu.VMEM((8, 8 * NC, 7 * 256), BF16),
                pltpu.VMEM((256, 256), BF16),
                pltpu.VMEM((n_gz, per, NC, 128), BF16),
                pltpu.VMEM((NRHS, NC, 128), BF16),
                pltpu.VMEM((ITERS, 2, 4, 2, NC, 128), BF16),
                pltpu.VMEM((ITERS, 2, 4, 2, NC, 128), BF16),
                pltpu.VMEM((ITERS, 2, 2, 2, NC, 128), BF16),
                pltpu.VMEM((4, 6, 2, NC, 128), BF16),
                pltpu.VMEM((GROUPS, NC, 128), F32),
                pltpu.VMEM((ITERS + 1, GROUPS, NC, 128), F32),
                pltpu.VMEM((GROUPS, NC, 128), F32),
                pltpu.VMEM((2, 2, 8 * NC, 128), F32),
                pltpu.VMEM((ITERS, first, 8, 128), F32),
                pltpu.VMEM((ITERS, second, 8, 128), F32),
                pltpu.VMEM((NRHS, NC, 128), BF16),
                pltpu.VMEM((n_gz, per, NC, 128), BF16),
                dma((SLOTS, 9)),
                dma((n_gz,)),
                dma((n_gz,)),
                dma((ITERS, 2, 4)),
                dma((ITERS, 2, 4)),
                dma((ITERS, 2)),
                dma((ITERS, 2)),
                dma((ITERS, first)),
                dma((ITERS, first)),
                dma((ITERS, second)),
                dma((ITERS, second)),
                dma((n_gz,)),
                dma((n_gz,)),
            ],
            compiler_params=pltpu.CompilerParams(
                collective_id=0, has_side_effects=True, vmem_limit_bytes=60 * 1024 * 1024
            ),
        )(restricted, mass_terms, clover_blocks, hop_links)
        return sol.astype(F32), res

    return jax.shard_map(
        step,
        mesh=mesh,
        in_specs=(
            P("gz", None, "ta"),
            P(None, ("ta", "gz")),
            P(None, None, ("ta", "gz")),
            P(None, None, None, ("ta", "gz")),
        ),
        out_specs=(P("gz", None, "ta"), P(None, None, ("ta", "gz"))),
        check_vma=False,
    )
```

time: 139 us -> 92.6 us (0.67)
  Pallas kernels: 134 us -> 87.7 us
  local copies, waits for them, and re-layouts: 4.16 us -> 2.07 us
  other arithmetic: 0 us -> 1.96 us
    pallas_call x1, Pallas kernels: 134 us -> 87.7 us  [step(): pl.pallas_call(functools.partial(kernel, n_ta, n_gz), out_shape=(jax.Shap...]
    unnamed x2 -> x1, local copies, waits for them, and re-layouts: 4.16 us -> 2.07 us
    convert_element_type x0 -> x1, other arithmetic: none -> 1.96 us  [step(): return (sol.astype(F32), res)]
where the time goes in v2:
time: 92.6 us; the launch traced here: 92.4 us
  Pallas kernels  87.7 us (95%)
  local copies, waits for them, and re-layouts  2.07 us (2%)
  other arithmetic  1.96 us (2%)
    pallas_call x1, Pallas kernels, step(): pl.pallas_call(functools.partial(kernel, n_ta, n_gz), out_shape=(jax.Shap...  87.7 us
    unnamed x1, local copies, waits for them, and re-layouts  2.07 us
    convert_element_type x1, other arithmetic, step(): return (sol.astype(F32), res)  1.96 us

profile of v2, /device:TPU:1, one launch (start us, length us, event | category | flops | bytes accessed | tf_op | source)
XLA Modules:
  0.0 92.4 jit_solution(4078065457425901876)
XLA Ops:
  0.6 87.7 %shard_map.59 = (bf16[2,96,1024]{2,1,0:T(8,128)(2,1)}, f32[16,96,128]{2,1,0:T(8,128)}) custom-call(f32[2,96,1024]{2,1,0:T(8,128)} %restricted.1, f32[96,128]{1,0:T(8,128)} %mass.1, bf16[96,96,128]{2,1,0:T(8,128)(2,1)} %clover.1, bf16[8,96,96,128]{3,2,1,0:T(8,128)(2,1)} %hops.1), custom_call_target="tpu_custom_call" | custom-call | tf_op jit(solution)/shard_map/pallas_call | solution.py:512
  88.3 2.0 %convert_element_type.3 = f32[2,96,1024]{2,1,0:T(8,128)} convert(bf16[2,96,1024]{2,1,0:T(8,128)(2,1)} %get-tuple-element.4) | non-fusion elementwise | flops 196608 | bytes 1179648 | tf_op jit(solution)/shard_map/convert_element_type | solution.py:556
  90.3 2.1 %copy.7 = f32[16,96,128]{2,1,0:T(8,128)} copy(f32[16,96,128]{2,1,0:T(8,128)} %get-tuple-element.9) | data formatting | bytes 1572864

commit v3 on v2

--- a/solution.py
+++ b/solution.py
@@ -15,6 +15,7 @@
 GROUPS = 16
 SLOTS = 6
 CHUNK = 8
+EARLY = 6
 SHIFT = 3.0
 F32 = jnp.float32
 BF16 = jnp.bfloat16
@@ -60,11 +61,11 @@
 
 def kernel(
     n_ta, n_gz,
-    restricted, mass, clover, hops,
+    restricted, mass_in, clover, hops,
     sol_out, res_out,
     links, matrix, perm, stage_in, field_in, own, halo_t, halo_z, ext, mass_f, basis, near, acc,
-    part1, part2, back_out, back_in,
-    link_sem, in_send, in_recv, t_send, t_recv, z_send, z_recv, s1_send, s1_recv, s2_send, s2_recv, out_send, out_recv,
+    part1, part2, back_out, back_in, rhs, mass, res_buf,
+    rhs_sem, mass_sem, res_sem, link_sem, in_send, in_recv, t_send, t_recv, z_send, z_recv, s1_send, s1_recv, s2_send, s2_recv, out_send, out_recv,
 ):
     ta = lax.axis_index("ta")
     gz = lax.axis_index("gz")
@@ -94,32 +95,21 @@
             )
         return copies
 
+    rhs_copy = pltpu.make_async_copy(restricted, rhs, rhs_sem)
+    rhs_copy.start()
+    mass_copy = pltpu.make_async_copy(mass_in, mass, mass_sem)
+    mass_copy.start()
     barrier = pltpu.get_barrier_semaphore()
     greet = [(ta, (gz + o) % n_gz) for o in range(1, n_gz)] + peers1 + peers2 + [(ta_up, gz), (ta_down, gz)]
     for to in greet:
         pl.semaphore_signal(barrier, inc=1, device_id=to, device_id_type=MESH)
 
+    rhs_copy.wait()
     for c in range(SLOTS):
         for copy in link_copies(c, c):
             copy.start()
-
     for b in range(n_gz):
-        stage_in[b] = restricted[:, :, 128 * b : 128 * b + 128].astype(BF16)
-    rows_i = lax.broadcasted_iota(jnp.int32, (256, 256), 0)
-    cols_i = lax.broadcasted_iota(jnp.int32, (256, 256), 1)
-    wanted = ((rows_i // 8) % 2) * 128 + (rows_i // 16) * 8 + rows_i % 8
-    perm[...] = jnp.where(cols_i == wanted, 1.0, 0.0).astype(BF16)
-
-    def mass_step(c, carry):
-        rows = pl.ds(pl.multiple_of(c * 16, 16), 16)
-        m = mass[rows, :] - SHIFT
-        spread = swap_blocks([m] * 16)
-        for g in range(GROUPS):
-            mass_f[g, rows, :] = spread[g]
-        return carry
-
-    lax.fori_loop(0, NC // 16, mass_step, 0, unroll=2)
-
+        stage_in[b] = rhs[:, :, 128 * b : 128 * b + 128].astype(BF16)
     pl.semaphore_wait(barrier, len(greet))
 
     def in_copy(o):
@@ -136,6 +126,22 @@
     for o in range(1, n_gz):
         in_copy(o).start()
     field_in[pl.ds(gz * per, per)] = stage_in[gz]
+
+    rows_i = lax.broadcasted_iota(jnp.int32, (256, 256), 0)
+    cols_i = lax.broadcasted_iota(jnp.int32, (256, 256), 1)
+    wanted = ((rows_i // 8) % 2) * 128 + (rows_i // 16) * 8 + rows_i % 8
+    perm[...] = jnp.where(cols_i == wanted, 1.0, 0.0).astype(BF16)
+
+    def mass_step(c, carry):
+        rows = pl.ds(pl.multiple_of(c * 16, 16), 16)
+        m = mass[rows, :] - SHIFT
+        spread = swap_blocks([m] * 16)
+        for g in range(GROUPS):
+            mass_f[g, rows, :] = spread[g]
+        return carry
+
+    mass_copy.wait()
+    lax.fori_loop(0, NC // 16, mass_step, 0, unroll=2)
 
     def prepare(c, carry):
         slot = c % SLOTS
@@ -183,8 +189,7 @@
             device_id=(ta, gz_down if side else gz_up), device_id_type=MESH,
         )
 
-    def send_halo(m, z):
-        t_copy(m, 0, z).start()
+    def send_rest(m, z):
         t_copy(m, 1, z).start()
 
         @pl.when(z == 0)
@@ -205,50 +210,90 @@
             parts.append(total)
         return jnp.concatenate(parts, axis=0)
 
+    def z_at(i):
+        return lax.rem(3 * i, 4)
+
+    def near_dot(k, mix, t, z):
+        lane = lanes(NC)
+
+        def packed(condition):
+            return jnp.where(condition, 1.0, 0.0).astype(BF16) > 0.5
+
+        low_x, not_last, not_first = packed((lane & 4) == 0), packed((lane & 3) < 3), packed((lane & 3) > 0)
+        pad = jnp.zeros((32, 128), BF16)
+        vs, swaps, sides = [], [], []
+        for half in range(2):
+            g = (t * 4 + z) * 2 + half
+            if k < ITERS - 1:
+                v = basis[k, g]
+            else:
+                v = mix[0] * basis[1, g]
+                for m in range(1, k):
+                    v = v + mix[m] * basis[m + 1, g]
+            near[g] = mass_f[g] * v
+            v = v.astype(BF16)
+            vs.append(v)
+            swaps.append(jnp.where(low_x, pltpu.roll(v, 124, 1), pltpu.roll(v, 4, 1)))
+        for half in range(2):
+            v, here, there = vs[half], swaps[half], swaps[1 - half]
+            ext[t + 1, z + 1, half] = v
+            pieces = [
+                v,
+                jnp.where(low_x, here, there),
+                jnp.where(low_x, there, here),
+                jnp.where(not_last, pltpu.roll(v, 127, 1), pltpu.roll(v, 3, 1)),
+                jnp.where(not_first, pltpu.roll(v, 1, 1), pltpu.roll(v, 125, 1)),
+                pad,
+            ]
+            sides.append(jnp.concatenate(pieces, axis=0))
+        out = jnp.dot(matrix[t * 4 + z, :, :1024], block_diagonal(*sides), preferred_element_type=F32)
+        acc[t, 0] = out[:, :128]
+        acc[t, 1] = out[:, 128:]
+
+    def near_take(t, z):
+        for half in range(2):
+            g = (t * 4 + z) * 2 + half
+            near[g] += chosen(t, half)
+
     def near_products(k, mix, i, carry):
-        z = lax.rem(3 * i, 4)
-        lane = lanes(NC)
-        low_x = (lane & 4) == 0
-        y = lane & 3
-        pad = jnp.zeros((32, 128), BF16)
-        for t in range(2):
-            vs, swaps, sides = [], [], []
-            for half in range(2):
-                g = (t * 4 + z) * 2 + half
-                if k < 2:
-                    v = basis[k, g]
-                else:
-                    v = mix[0] * basis[1, g]
-                    for m in range(1, k):
-                        v = v + mix[m] * basis[m + 1, g]
-                vs.append(v)
-                swaps.append(jnp.where(low_x, pltpu.roll(v, 124, 1), pltpu.roll(v, 4, 1)))
-            for half in range(2):
-                v, here, there = vs[half], swaps[half], swaps[1 - half]
-                center = v.astype(BF16)
-                ext[t + 1, z + 1, half] = center
-                pieces = [
-                    center,
-                    jnp.where(low_x, here, there).astype(BF16),
-                    jnp.where(low_x, there, here).astype(BF16),
-                    jnp.where(y < 3, pltpu.roll(v, 127, 1), pltpu.roll(v, 3, 1)).astype(BF16),
-                    jnp.where(y > 0, pltpu.roll(v, 1, 1), pltpu.roll(v, 125, 1)).astype(BF16),
-                    pad,
-                ]
-                sides.append(jnp.concatenate(pieces, axis=0))
-            out = jnp.dot(matrix[t * 4 + z, :, :1024], block_diagonal(*sides), preferred_element_type=F32)
-            acc[t, 0] = out[:, :128]
-            acc[t, 1] = out[:, 128:]
-            for half in range(2):
-                g = (t * 4 + z) * 2 + half
-                near[g] = chosen(t, half) + mass_f[g] * vs[half]
+        near_dot(k, mix, 0, z_at(i))
+        near_take(1, z_at(i + 3))
+        near_dot(k, mix, 1, z_at(i))
+        near_take(0, z_at(i))
         return carry
 
+    def far_dot(t, z):
+        sides = []
+        for half in range(2):
+            pieces = [
+                ext[t + 1, z + 2, half], ext[t + 1, z, half], ext[t + 2, z + 1, half], ext[t, z + 1, half]
+            ]
+            sides.append(jnp.concatenate(pieces, axis=0))
+        out = jnp.dot(matrix[t * 4 + z, :, 1024:], block_diagonal(*sides), preferred_element_type=F32)
+        acc[t, 0] = out[:, :128]
+        acc[t, 1] = out[:, 128:]
+
+    def far_take(k, t, z):
+        sums = None
+        for half in range(2):
+            g = (t * 4 + z) * 2 + half
+            new = near[g] + chosen(t, half)
+            basis[k + 1, g] = new
+            if k < ITERS - 1:
+                own[k + 1, t, z, half] = new.astype(BF16)
+            others = [basis[j, g] for j in range(k + 1)]
+            products = [other * new for other in others] + [new * new]
+            if k == 0:
+                products.append(others[0] * others[0])
+            part = [jnp.sum(product.reshape(NC // 8, 8, 128), axis=0) for product in products]
+            sums = part if sums is None else [a + b for a, b in zip(sums, part)]
+        return sums
+
     def far_products(k, mix, i, carry):
-        z = lax.rem(3 * i, 4)
+        z = z_at(i)
 
         def mixed(ref, *at):
-            if k < 2:
+            if k < ITERS - 1:
                 return ref[(k, *at)]
             v = mix[0] * ref[(1, *at)].astype(F32)
             for m in range(1, k):
@@ -269,32 +314,24 @@
                     for half in range(2):
                         ext[t + 1, 5 * side, half] = mixed(halo_z, side, t, half)
 
-        carry = list(carry)
-        for t in range(2):
-            sides = []
-            for half in range(2):
-                pieces = [
-                    ext[t + 1, z + 2, half], ext[t + 1, z, half], ext[t + 2, z + 1, half], ext[t, z + 1, half]
-                ]
-                sides.append(jnp.concatenate(pieces, axis=0))
-            out = jnp.dot(matrix[t * 4 + z, :, 1024:], block_diagonal(*sides), preferred_element_type=F32)
-            acc[t, 0] = out[:, :128]
-            acc[t, 1] = out[:, 128:]
-            for half in range(2):
-                g = (t * 4 + z) * 2 + half
-                new = near[g] + chosen(t, half)
-                basis[k + 1, g] = new
-                if k < ITERS - 1:
-                    own[k + 1, t, z, half] = new.astype(BF16)
-                others = [basis[j, g] for j in range(k + 1)]
-                products = [other * new for other in others] + [new * new]
-                if k == 0:
-                    products.append(others[0] * others[0])
-                for j, product in enumerate(products):
-                    carry[j] = carry[j] + jnp.sum(product.reshape(NC // 8, 8, 128), axis=0)
+        if k == 2:
+
+            @pl.when(i == 1)
+            def _():
+                sum_middle(0)
+
+        far_dot(0, z)
+        before = far_take(k, 1, z_at(i + 3))
+        far_dot(1, z)
+        now = far_take(k, 0, z)
         if k < ITERS - 1:
-            send_halo(k + 1, z)
-        return tuple(carry)
+            t_copy(k + 1, 0, z).start()
+
+            @pl.when(i > 0)
+            def _():
+                send_rest(k + 1, z_at(i + 3))
+
+        return tuple(c + jnp.where(i > 0, b, 0.0) + n for c, b, n in zip(carry, before, now))
 
     def share(number, stage):
         buf, place, peers, send, recv = (
@@ -332,7 +369,7 @@
             value = value + part2[number, n]
         return sum_sites(value)
 
-    lax.fori_loop(0, 6, prepare, 0)
+    lax.fori_loop(0, EARLY, prepare, 0)
     for o in range(1, n_gz):
         in_copy(o).wait_recv()
 
@@ -350,7 +387,7 @@
         t_copy(0, 1, z).start()
     z_copy(0, 1).start()
     z_copy(0, 0).start()
-    lax.fori_loop(6, NC // CHUNK, prepare, 0)
+    lax.fori_loop(EARLY, NC // CHUNK, prepare, 0)
 
     size = ITERS + 1
     gram = {}
@@ -405,9 +442,10 @@
         qo, po = scale(inverse, qo), scale(inverse, po)
         x = add(x, alpha, po)
         if k < ITERS - 1:
-            bq = add(unit(k + 2), SHIFT, p)
-            for beta, product in zip(betas, image_products):
-                bq = add(bq, -beta, product)
+            product = [None] + p[:-1] if k == 1 else unit(k + 2)
+            bq = add(product, SHIFT, p)
+            for beta, earlier in zip(betas, image_products):
+                bq = add(bq, -beta, earlier)
             bq = scale(inverse, bq)
             image_products.append(bq)
             p = add(p, -alpha, bq)
@@ -416,30 +454,34 @@
         searches.append(po)
         return r, p, x
 
-    def take_gram(k, value):
-        for j in range(k + 2):
-            gram[j, k + 1] = gram[k + 1, j] = value[j : j + 1]
-        if k == 0:
-            gram[0, 0] = value[2:3]
-            gram[0, 1] = gram[1, 0] = value[0:1]
-            gram[1, 1] = value[1:2]
-
+    def take_gram(pairs, value):
+        for n, (i, j) in enumerate(pairs):
+            gram[i, j] = gram[j, i] = value[n : n + 1]
+
+    pairs, rows = [], []
     for k in range(ITERS):
         lax.fori_loop(0, 4, functools.partial(near_products, k, mix), 0)
-        if k > 0:
-            sum_middle(k - 1)
-        count = k + 2 + (k == 0)
+        near_take(1, z_at(3))
+        new_pairs = [(j, k + 1) for j in range(k + 2)] + ([(0, 0)] if k == 0 else [])
         zero = jnp.zeros((8, 128), F32)
-        sums = lax.fori_loop(0, 4, functools.partial(far_products, k, mix), (zero,) * count)
-        rows = [jnp.sum(v, axis=0, keepdims=True) for v in sums]
-        sum_start(k, jnp.concatenate(rows + [jnp.zeros((8 - count, 128), F32)], axis=0))
-        if k > 0:
-            take_gram(k - 1, sum_end(k - 1))
-            r, p, x = iterate(k - 1, r, p, x)
-            mix = p[1 : k + 2]
-    sum_middle(ITERS - 1)
-    take_gram(ITERS - 1, sum_end(ITERS - 1))
-    r, p, x = iterate(ITERS - 1, r, p, x)
+        sums = lax.fori_loop(0, 4, functools.partial(far_products, k, mix), (zero,) * len(new_pairs))
+        sums = [a + b for a, b in zip(sums, far_take(k, 1, z_at(3)))]
+        pairs += new_pairs
+        rows += [jnp.sum(v, axis=0, keepdims=True) for v in sums]
+        if k % 2:
+            sum_start(k // 2, jnp.concatenate(rows + [jnp.zeros((16 - len(rows), 128), F32)], axis=0))
+            sent, pairs, rows = pairs, [], []
+        if k < ITERS - 1:
+            t_copy(k + 1, 1, z_at(3)).start()
+        if k == 2:
+            take_gram(sent, sum_end(0))
+            for n in range(2):
+                r, p, x = iterate(n, r, p, x)
+            mix = p[1:4]
+    sum_middle(1)
+    take_gram(sent, sum_end(1))
+    for n in range(2, ITERS):
+        r, p, x = iterate(n, r, p, x)
 
     def combine(coefs, g, rows):
         total = None
@@ -477,10 +519,12 @@
         rows = pl.ds(pl.multiple_of(c * 16, 16), 16)
         xs = swap_blocks([combine(r, g, rows) for g in range(GROUPS)])
         for n in range(NRHS):
-            res_out[n, rows, :] = xs[n]
+            res_buf[n, rows, :] = xs[n]
         return carry
 
     lax.fori_loop(0, NC // 16, last_residual, 0, unroll=2)
+    res_copy = pltpu.make_async_copy(res_buf, res_out, res_sem)
+    res_copy.start()
 
     for o in range(1, n_gz):
         in_copy(o).wait_send()
@@ -490,13 +534,20 @@
             t_copy(m, 1, z).wait_send()
         z_copy(m, 0).wait_send()
         z_copy(m, 1).wait_send()
+    for number in range(2):
         for stage in range(2):
-            for copy in share(m, stage):
+            for copy in share(number, stage):
                 copy.wait_send()
     for o in range(1, n_gz):
         out_copy(o).wait()
     for b in range(n_gz):
         sol_out[:, :, 128 * b : 128 * b + 128] = back_in[b]
+    res_copy.wait()
+
+
+def deliver(sol, res, sol_out, res_out):
+    sol_out[...] = sol[...].astype(F32)
+    res_out[...] = res[...]
 
 
 def solution(mesh):
@@ -515,8 +566,8 @@
                 jax.ShapeDtypeStruct((per, NC, LOC * n_gz), BF16),
                 jax.ShapeDtypeStruct((NRHS, NC, LOC), F32),
             ),
-            in_specs=[vmem, vmem, hbm, hbm],
-            out_specs=(vmem, vmem),
+            in_specs=[hbm] * 4,
+            out_specs=(vmem, hbm),
             scratch_shapes=[
                 pltpu.VMEM((SLOTS, CHUNK, 9, NC, 128), BF16),
                 pltpu.VMEM((8, 8 * NC, 7 * 256), BF16),
@@ -531,10 +582,16 @@
                 pltpu.VMEM((ITERS + 1, GROUPS, NC, 128), F32),
                 pltpu.VMEM((GROUPS, NC, 128), F32),
                 pltpu.VMEM((2, 2, 8 * NC, 128), F32),
-                pltpu.VMEM((ITERS, first, 8, 128), F32),
-                pltpu.VMEM((ITERS, second, 8, 128), F32),
+                pltpu.VMEM((2, first, 16, 128), F32),
+                pltpu.VMEM((2, second, 16, 128), F32),
                 pltpu.VMEM((NRHS, NC, 128), BF16),
                 pltpu.VMEM((n_gz, per, NC, 128), BF16),
+                pltpu.VMEM((per, NC, LOC * n_gz), F32),
+                pltpu.VMEM((NC, LOC), F32),
+                pltpu.VMEM((NRHS, NC, LOC), F32),
+                dma,
+                dma,
+                dma,
                 dma((SLOTS, 9)),
                 dma((n_gz,)),
                 dma((n_gz,)),
@@ -542,10 +599,10 @@
                 dma((ITERS, 2, 4)),
                 dma((ITERS, 2)),
                 dma((ITERS, 2)),
-                dma((ITERS, first)),
-                dma((ITERS, first)),
-                dma((ITERS, second)),
-                dma((ITERS, second)),
+                dma((2, first)),
+                dma((2, first)),
+                dma((2, second)),
+                dma((2, second)),
                 dma((n_gz,)),
                 dma((n_gz,)),
             ],
@@ -553,7 +610,15 @@
                 collective_id=0, has_side_effects=True, vmem_limit_bytes=60 * 1024 * 1024
             ),
         )(restricted, mass_terms, clover_blocks, hop_links)
-        return sol.astype(F32), res
+        return pl.pallas_call(
+            deliver,
+            out_shape=(
+                jax.ShapeDtypeStruct((per, NC, LOC * n_gz), F32),
+                jax.ShapeDtypeStruct((NRHS, NC, LOC), F32),
+            ),
+            in_specs=[vmem, vmem],
+            out_specs=(vmem, vmem),
+        )(sol, res)
 
     return jax.shard_map(
         step,

time: 92.6 us -> 85.5 us (0.923)
  Pallas kernels: 87.7 us -> 84.5 us
  local copies, waits for them, and re-layouts: 2.07 us -> 0 us
  other arithmetic: 1.96 us -> 0 us
    pallas_call x1, Pallas kernels: 87.7 us -> 82.1 us  [step(): pl.pallas_call(functools.partial(kernel, n_ta, n_gz), out_shape=(jax.Shap...]
    pallas_call x0 -> x1, Pallas kernels: none -> 2.46 us  [step(): pl.pallas_call(deliver, out_shape=(jax.ShapeDtypeStruct((per, NC, LOC * n...]
    unnamed x1 -> x0, local copies, waits for them, and re-layouts: 2.07 us -> none
    convert_element_type x1 -> x0, other arithmetic: 1.96 us -> none  [step(): return (sol.astype(F32), res)]
where the time goes in v3:
time: 85.5 us; the launch traced here: 85.2 us
  Pallas kernels  84.5 us (99%)
    pallas_call x1, Pallas kernels, step(): pl.pallas_call(functools.partial(kernel, n_ta, n_gz), out_shape=(jax.Shap...  82.1 us
    pallas_call x1, Pallas kernels, step(): pl.pallas_call(deliver, out_shape=(jax.ShapeDtypeStruct((per, NC, LOC * n...  2.46 us

profile of v3, /device:TPU:1, one launch (start us, length us, event | category | flops | bytes accessed | tf_op | source)
XLA Modules:
  0.0 85.2 jit_solution(636031463534671717)
XLA Ops:
  0.6 82.1 %shard_map.59 = (bf16[2,96,1024]{2,1,0:T(8,128)(2,1)}, f32[16,96,128]{2,1,0:T(8,128)}) custom-call(f32[2,96,1024]{2,1,0:T(8,128)} %restricted.1, f32[96,128]{1,0:T(8,128)} %mass_in.1, bf16[96,96,128]{2,1,0:T(8,128)(2,1)} %clover.1, bf16[8,96,96,128]{3,2,1,0:T(8,128)(2,1)} %hops.1), custom_call_target="tpu_custom_call" | custom-call | tf_op jit(solution)/shard_map/pallas_call | solution.py:563
  82.7 2.5 %shard_map.60 = (f32[2,96,1024]{2,1,0:T(8,128)}, f32[16,96,128]{2,1,0:T(8,128)}) custom-call(bf16[2,96,1024]{2,1,0:T(8,128)(2,1)} %get-tuple-element.4.sol, f32[16,96,128]{2,1,0:T(8,128)} %get-tuple-element.5.res), custom_call_target="tpu_custom_call" | custom-call | tf_op jit(solution)/shard_map/pallas_call | solution.py:613

commit v4 on v3

--- a/solution.py
+++ b/solution.py
@@ -25,11 +25,17 @@
     return lax.broadcasted_iota(jnp.int32, (rows, 128), 1)
 
 
+def mask_for(dtype, condition):
+    if dtype == F32:
+        return condition
+    return jnp.where(condition, 1.0, 0.0).astype(BF16) > 0.5
+
+
 def swap_blocks(xs):
     lane = lanes(xs[0].shape[0])
     for b in (1, 2, 4, 8):
         shift = 8 * b
-        high = (lane & shift) != 0
+        high = mask_for(xs[0].dtype, (lane & shift) != 0)
         new = list(xs)
         for r in range(16):
             if r & b == 0:
@@ -100,7 +106,7 @@
     mass_copy = pltpu.make_async_copy(mass_in, mass, mass_sem)
     mass_copy.start()
     barrier = pltpu.get_barrier_semaphore()
-    greet = [(ta, (gz + o) % n_gz) for o in range(1, n_gz)] + peers1 + peers2 + [(ta_up, gz), (ta_down, gz)]
+    greet = peers2 + [(ta, (gz + o) % n_gz) for o in range(1, n_gz)] + [(ta_up, gz), (ta_down, gz)] + peers1
     for to in greet:
         pl.semaphore_signal(barrier, inc=1, device_id=to, device_id_type=MESH)
 
@@ -215,11 +221,9 @@
 
     def near_dot(k, mix, t, z):
         lane = lanes(NC)
-
-        def packed(condition):
-            return jnp.where(condition, 1.0, 0.0).astype(BF16) > 0.5
-
-        low_x, not_last, not_first = packed((lane & 4) == 0), packed((lane & 3) < 3), packed((lane & 3) > 0)
+        low_x = mask_for(BF16, (lane & 4) == 0)
+        not_last = mask_for(BF16, (lane & 3) < 3)
+        not_first = mask_for(BF16, (lane & 3) > 0)
         pad = jnp.zeros((32, 128), BF16)
         vs, swaps, sides = [], [], []
         for half in range(2):
@@ -375,13 +379,13 @@
 
     def arrange(c, carry):
         rows = pl.ds(pl.multiple_of(c * 16, 16), 16)
-        xs = swap_blocks([field_in[r, rows, :].astype(F32) for r in range(NRHS)])
+        xs = swap_blocks([field_in[r, rows, :] for r in range(NRHS)])
         for g in range(GROUPS):
-            basis[0, g, rows, :] = xs[g]
-            own[0, g // 8, (g // 2) % 4, g % 2, rows, :] = xs[g].astype(BF16)
+            own[0, g // 8, (g // 2) % 4, g % 2, rows, :] = xs[g]
+            basis[0, g, rows, :] = xs[g].astype(F32)
         return carry
 
-    lax.fori_loop(0, NC // 16, arrange, 0, unroll=2)
+    lax.fori_loop(0, NC // 16, arrange, 0, unroll=3)
     for z in range(4):
         t_copy(0, 0, z).start()
         t_copy(0, 1, z).start()
@@ -493,12 +497,12 @@
 
     def finish(c, carry):
         rows = pl.ds(pl.multiple_of(c * 16, 16), 16)
-        xs = swap_blocks([combine(x, g, rows) for g in range(GROUPS)])
+        xs = swap_blocks([combine(x, g, rows).astype(BF16) for g in range(GROUPS)])
         for n in range(NRHS):
-            back_out[n, rows, :] = xs[n].astype(BF16)
+            back_out[n, rows, :] = xs[n]
         return carry
 
-    lax.fori_loop(0, NC // 16, finish, 0, unroll=2)
+    lax.fori_loop(0, NC // 16, finish, 0, unroll=3)
 
     def out_copy(o):
         to = (gz + o) % n_gz
@@ -545,9 +549,31 @@
     res_copy.wait()
 
 
-def deliver(sol, res, sol_out, res_out):
-    sol_out[...] = sol[...].astype(F32)
-    res_out[...] = res[...]
+PIECES = 3
+
+
+def deliver(sol, res, sol_out, res_out, narrow, wide, held, in_sem, out_sem):
+    def piece(n, size):
+        return pl.ds(n * (size // PIECES), size // PIECES)
+
+    a = [piece(n, NC) for n in range(PIECES)]
+    b = [pl.ds(*at) for at in ((0, 6), (6, 6), (12, 4))]
+    fetch, store = [], []
+    for n in range(PIECES):
+        fetch.append(pltpu.make_async_copy(sol.at[:, a[n]], narrow.at[n], in_sem.at[0, n]))
+        fetch.append(pltpu.make_async_copy(res.at[b[n]], held.at[b[n]], in_sem.at[1, n]))
+        store.append(pltpu.make_async_copy(wide.at[n], sol_out.at[:, a[n]], out_sem.at[0, n]))
+        store.append(pltpu.make_async_copy(held.at[b[n]], res_out.at[b[n]], out_sem.at[1, n]))
+    for copy in fetch:
+        copy.start()
+    for n in range(PIECES):
+        fetch[2 * n].wait()
+        wide[n] = narrow[n].astype(F32)
+        store[2 * n].start()
+        fetch[2 * n + 1].wait()
+        store[2 * n + 1].start()
+    for copy in store:
+        copy.wait()
 
 
 def solution(mesh):
@@ -616,8 +642,15 @@
                 jax.ShapeDtypeStruct((per, NC, LOC * n_gz), F32),
                 jax.ShapeDtypeStruct((NRHS, NC, LOC), F32),
             ),
-            in_specs=[vmem, vmem],
-            out_specs=(vmem, vmem),
+            in_specs=[hbm, hbm],
+            out_specs=(hbm, hbm),
+            scratch_shapes=[
+                pltpu.VMEM((PIECES, per, NC // PIECES, LOC * n_gz), BF16),
+                pltpu.VMEM((PIECES, per, NC // PIECES, LOC * n_gz), F32),
+                pltpu.VMEM((NRHS, NC, LOC), F32),
+                dma((2, PIECES)),
+                dma((2, PIECES)),
+            ],
         )(sol, res)
 
     return jax.shard_map(

time: 85.5 us -> 84.9 us (level)
  no operation moved by 1% of the time
where the time goes in v4:
time: 84.9 us; the launch traced here: 84.8 us
  Pallas kernels  84.1 us (99%)
    pallas_call x1, Pallas kernels, step(): pl.pallas_call(functools.partial(kernel, n_ta, n_gz), out_shape=(jax.Shap...  81.9 us
    pallas_call x1, Pallas kernels, step(): pl.pallas_call(deliver, out_shape=(jax.ShapeDtypeStruct((per, NC, LOC * n...  2.18 us

profile of v4, /device:TPU:1, one launch (start us, length us, event | category | flops | bytes accessed | tf_op | source)
XLA Modules:
  0.0 84.8 jit_solution(16828244179068157932)
XLA Ops:
  0.6 81.9 %shard_map.59 = (bf16[2,96,1024]{2,1,0:T(8,128)(2,1)}, f32[16,96,128]{2,1,0:T(8,128)}) custom-call(f32[2,96,1024]{2,1,0:T(8,128)} %restricted.1, f32[96,128]{1,0:T(8,128)} %mass_in.1, bf16[96,96,128]{2,1,0:T(8,128)(2,1)} %clover.1, bf16[8,96,96,128]{3,2,1,0:T(8,128)(2,1)} %hops.1), custom_call_target="tpu_custom_call" | custom-call | tf_op jit(solution)/shard_map/pallas_call | solution.py:589
  82.6 2.2 %shard_map.60 = (f32[2,96,1024]{2,1,0:T(8,128)}, f32[16,96,128]{2,1,0:T(8,128)}) custom-call(bf16[2,96,1024]{2,1,0:T(8,128)(2,1)} %get-tuple-element.4.sol, f32[16,96,128]{2,1,0:T(8,128)} %get-tuple-element.5.res), custom_call_target="tpu_custom_call" | custom-call | tf_op jit(solution)/shard_map/pallas_call | solution.py:639

commit v5 on v4

--- a/solution.py
+++ b/solution.py
@@ -458,6 +458,30 @@
         searches.append(po)
         return r, p, x
 
+    def out_copy(m, o):
+        to = (gz + o) % n_gz
+        return pltpu.make_async_remote_copy(
+            src_ref=back_out.at[m - 1, pl.ds(to * per, per)],
+            dst_ref=back_in.at[m - 1, gz],
+            send_sem=out_send.at[m - 1, o],
+            recv_sem=out_recv.at[m - 1, o],
+            device_id=(ta, to),
+            device_id_type=MESH,
+        )
+
+    def send_back(m):
+        def turn(c, carry):
+            rows = pl.ds(pl.multiple_of(c * 16, 16), 16)
+            xs = swap_blocks([own[m, g // 8, (g // 2) % 4, g % 2, rows, :] for g in range(GROUPS)])
+            for n in range(NRHS):
+                back_out[m - 1, n, rows, :] = xs[n]
+            return carry
+
+        lax.fori_loop(0, NC // 16, turn, 0, unroll=3)
+        for o in range(1, n_gz):
+            out_copy(m, o).start()
+        back_in[m - 1, gz] = back_out[m - 1, pl.ds(gz * per, per)]
+
     def take_gram(pairs, value):
         for n, (i, j) in enumerate(pairs):
             gram[i, j] = gram[j, i] = value[n : n + 1]
@@ -482,6 +506,8 @@
             for n in range(2):
                 r, p, x = iterate(n, r, p, x)
             mix = p[1:4]
+            for m in range(1, ITERS):
+                send_back(m)
     sum_middle(1)
     take_gram(sent, sum_end(1))
     for n in range(2, ITERS):
@@ -494,30 +520,6 @@
                 term = c * basis[m, g, rows, :]
                 total = term if total is None else total + term
         return total
-
-    def finish(c, carry):
-        rows = pl.ds(pl.multiple_of(c * 16, 16), 16)
-        xs = swap_blocks([combine(x, g, rows).astype(BF16) for g in range(GROUPS)])
-        for n in range(NRHS):
-            back_out[n, rows, :] = xs[n]
-        return carry
-
-    lax.fori_loop(0, NC // 16, finish, 0, unroll=3)
-
-    def out_copy(o):
-        to = (gz + o) % n_gz
-        return pltpu.make_async_remote_copy(
-            src_ref=back_out.at[pl.ds(to * per, per)],
-            dst_ref=back_in.at[gz],
-            send_sem=out_send.at[o],
-            recv_sem=out_recv.at[o],
-            device_id=(ta, to),
-            device_id_type=MESH,
-        )
-
-    for o in range(1, n_gz):
-        out_copy(o).start()
-    back_in[gz] = back_out[pl.ds(gz * per, per)]
 
     def last_residual(c, carry):
         rows = pl.ds(pl.multiple_of(c * 16, 16), 16)
@@ -542,10 +544,17 @@
         for stage in range(2):
             for copy in share(number, stage):
                 copy.wait_send()
-    for o in range(1, n_gz):
-        out_copy(o).wait()
-    for b in range(n_gz):
-        sol_out[:, :, 128 * b : 128 * b + 128] = back_in[b]
+    for m in range(1, ITERS):
+        for o in range(1, n_gz):
+            out_copy(m, o).wait()
+    for n in range(per):
+        mine = lanes(1) == 8 * (gz * per + n)
+        parts = [jnp.sum(jnp.where(mine, x[m], 0.0), axis=1, keepdims=True) for m in range(ITERS)]
+        for b in range(n_gz):
+            total = parts[0] * stage_in[b, n].astype(F32)
+            for m in range(1, ITERS):
+                total = total + parts[m] * back_in[m - 1, b, n].astype(F32)
+            sol_out[n, :, 128 * b : 128 * b + 128] = total.astype(BF16)
     res_copy.wait()
 
 
@@ -610,8 +619,8 @@
                 pltpu.VMEM((2, 2, 8 * NC, 128), F32),
                 pltpu.VMEM((2, first, 16, 128), F32),
                 pltpu.VMEM((2, second, 16, 128), F32),
-                pltpu.VMEM((NRHS, NC, 128), BF16),
-                pltpu.VMEM((n_gz, per, NC, 128), BF16),
+                pltpu.VMEM((ITERS - 1, NRHS, NC, 128), BF16),
+                pltpu.VMEM((ITERS - 1, n_gz, per, NC, 128), BF16),
                 pltpu.VMEM((per, NC, LOC * n_gz), F32),
                 pltpu.VMEM((NC, LOC), F32),
                 pltpu.VMEM((NRHS, NC, LOC), F32),
@@ -629,8 +638,8 @@
                 dma((2, first)),
                 dma((2, second)),
                 dma((2, second)),
-                dma((n_gz,)),
-                dma((n_gz,)),
+                dma((ITERS - 1, n_gz)),
+                dma((ITERS - 1, n_gz)),
             ],
             compiler_params=pltpu.CompilerParams(
                 collective_id=0, has_side_effects=True, vmem_limit_bytes=60 * 1024 * 1024

time: 84.9 us -> 86.7 us (1.021)
  Pallas kernels: 84.1 us -> 86 us
    pallas_call x1, Pallas kernels: 81.9 us -> 83.8 us  [step(): pl.pallas_call(functools.partial(kernel, n_ta, n_gz), out_shape=(jax.Shap...]
where the time goes in v5:
time: 86.7 us; the launch traced here: 86.6 us
  Pallas kernels  86 us (99%)
    pallas_call x1, Pallas kernels, step(): pl.pallas_call(functools.partial(kernel, n_ta, n_gz), out_shape=(jax.Shap...  83.8 us
    pallas_call x1, Pallas kernels, step(): pl.pallas_call(deliver, out_shape=(jax.ShapeDtypeStruct((per, NC, LOC * n...  2.18 us

profile of v5, /device:TPU:1, one launch (start us, length us, event | category | flops | bytes accessed | tf_op | source)
XLA Modules:
  0.0 86.6 jit_solution(1520039770213913848)
XLA Ops:
  0.6 83.8 %shard_map.59 = (bf16[2,96,1024]{2,1,0:T(8,128)(2,1)}, f32[16,96,128]{2,1,0:T(8,128)}) custom-call(f32[2,96,1024]{2,1,0:T(8,128)} %restricted.1, f32[96,128]{1,0:T(8,128)} %mass_in.1, bf16[96,96,128]{2,1,0:T(8,128)(2,1)} %clover.1, bf16[8,96,96,128]{3,2,1,0:T(8,128)(2,1)} %hops.1), custom_call_target="tpu_custom_call" | custom-call | tf_op jit(solution)/shard_map/pallas_call | solution.py:598
  84.4 2.2 %shard_map.60 = (f32[2,96,1024]{2,1,0:T(8,128)}, f32[16,96,128]{2,1,0:T(8,128)}) custom-call(bf16[2,96,1024]{2,1,0:T(8,128)(2,1)} %get-tuple-element.4.sol, f32[16,96,128]{2,1,0:T(8,128)} %get-tuple-element.5.res), custom_call_target="tpu_custom_call" | custom-call | tf_op jit(solution)/shard_map/pallas_call | solution.py:648
